TPU v7x, 32 devices: a whole 2x2x4 slice. The times are simulated.
32 devices in a mesh: gx: 4 (over z), gy: 2 (over y), gz: 4 (over x, core).
Axes of the slice: x: 2, y: 2, z: 4, core: 2. Of those that a mesh axis runs over, the one named last changes fastest.
Arguments:
- right_side: float32 [4, 2, 4, 6, 1024], P('gx', 'gy', 'gz'), may hold values from -18 to 18
- grain_diag: float32 [4, 2, 4, 6, 1024], P('gx', 'gy', 'gz'), may hold values from 0.05 to 0.5
- stiffness: float32 [4, 4], replicated, may hold values from 0.3 to 3
- contact_own: int32 [4, 2, 4, 3072], P('gx', 'gy', 'gz'), may hold values from 0 to 1023, as said below
- contact_slot: int32 [4, 2, 4, 3072], P('gx', 'gy', 'gz'), may hold values from 0 to 7679, as said below
- contact_type: int32 [4, 2, 4, 3072], P('gx', 'gy', 'gz'), may hold values from 0 to 4, as said below
- contact_normal: float32 [4, 2, 4, 3, 3072], P('gx', 'gy', 'gz'), may hold values from -1 to 1, as said below
- contact_radii: float32 [4, 2, 4, 2, 3072], P('gx', 'gy', 'gz'), may hold values from 0.4 to 1
Outputs:
- solution_field: float32 [4, 2, 4, 6, 1024], P('gx', 'gy', 'gz')
- residual: float32 [4, 2, 4, 6, 1024], P('gx', 'gy', 'gz')
Inputs may be any that keep to these rules, and one draw needn't show every extreme that they name: `contact_normal`: each normal has unit length. `contact_own`: in the first 2240 slots of a block the own grain differs from the partner; in the last 832 slots the own grain is one of the block's first 256 grains. `contact_slot`: the first 2240 slots of a block hold values below 1024; the slots 3072 - 832 + k * 32 to 2240 + (k + 1) * 32 - 1, for k = 0 to 25, hold values from 1024 + k * 256 to 1024 + (k + 1) * 256 - 1. `contact_type`: the value 4 marks an empty slot.
All inputs are finite; a program needn't handle non-finite values.
Results may differ from a plain program's by a relative error of at most 0.00018.
Values sent between devices are 32-bit elements; how exact they have to be, the bound alone decides.
No kernel may reach another device: no remote copies, remote signals or barrier semaphores. Data moves between devices by JAX's collectives and lax.ppermute only.
A program may use at most 64 MiB of HBM per device.

v0:
```python
import functools

import jax
import jax.numpy as jnp
from jax import lax
from jax.experimental import pallas as pl
from jax.experimental.pallas import tpu as pltpu
from jax.sharding import PartitionSpec as P

ITERS = 4
AXES = ("gx", "gy", "gz")
LANES = 128
FIELDS = 6


class Plan:
    def __init__(self, mesh, grains, contacts, types):
        self.counts = tuple(mesh.shape[axis] for axis in AXES)
        self.devices = self.counts[0] * self.counts[1] * self.counts[2]
        self.grains = grains
        self.rim = grains // 4
        self.group = grains // 32
        self.contacts = contacts
        self.types = types
        self.near = contacts - 26 * self.group
        self.near_tiles = -(-self.near // LANES)
        self.tiles = contacts // LANES
        self.grain_tiles = grains // LANES
        self.rim_tiles = self.rim // LANES
        sides = {}
        for k in range(26):
            whole = k + (1 if k >= 13 else 0)
            offset = (whole // 9 - 1, whole // 3 % 3 - 1, whole % 3 - 1)
            delta = tuple(o % c for o, c in zip(offset, self.counts))
            sides.setdefault(delta, []).append(k)
        self.sides = sorted(sides.items())
        self.far = len(self.sides)
        most = max(len(groups) for groups in sides.values())
        self.half = -(-most * self.group // (LANES // 2)) * (LANES // 2)
        assert self.half * 2 == LANES

    def neighbours(self):
        place = [lax.axis_index(axis) for axis in AXES]
        found = []
        for delta, _ in self.sides:
            x, y, z = (lax.rem(p + d, c) for p, d, c in zip(place, delta, self.counts))
            found.append((x * self.counts[1] + y) * self.counts[2] + z)
        return found


def row_of(ref, row, stride, count):
    return ref[pl.ds(row, count, stride=stride), :]


def lane_gather(tiles, index):
    low = jnp.bitwise_and(index, LANES - 1)
    high = lax.shift_right_logical(index, 7)
    total = jnp.zeros(tiles[0].shape, tiles[0].dtype)
    for which, tile in enumerate(tiles):
        found = jnp.take_along_axis(tile, low, axis=1, mode="promise_in_bounds")
        total = jnp.where(high == which, found, total)
    return total


def spread(ref, row):
    return jnp.broadcast_to(ref[row : row + 1, :], (8, LANES))


def coefficients(stiff_ref, kind, types, valid=None):
    found = []
    for which in range(4):
        total = jnp.zeros(kind.shape, jnp.float32)
        for t in range(types):
            total = jnp.where(kind == t, stiff_ref[which : which + 1, t : t + 1], total)
        if valid is not None:
            total = jnp.where(valid, total, 0.0)
        found.append(total)
    normal_k, shear_k, roll_k, twist_k = found
    return shear_k, normal_k - shear_k, roll_k, twist_k - roll_k


def response(first, second, table):
    n = table[0:3]
    first_r, second_r, shear_k, normal_d, roll_k, twist_d = table[3:]
    p = [second_r * second[3 + c] + first_r * first[3 + c] for c in range(3)]
    delta = []
    for c in range(3):
        a, b = (c + 1) % 3, (c + 2) % 3
        delta.append(second[c] - first[c] - (p[a] * n[b] - p[b] * n[a]))
    theta = [second[3 + c] - first[3 + c] for c in range(3)]
    along = normal_d * (n[0] * delta[0] + n[1] * delta[1] + n[2] * delta[2])
    twist = twist_d * (n[0] * theta[0] + n[1] * theta[1] + n[2] * theta[2])
    force = [shear_k * delta[c] + along * n[c] for c in range(3)]
    moment = [roll_k * theta[c] + twist * n[c] for c in range(3)]
    lever = []
    for c in range(3):
        a, b = (c + 1) % 3, (c + 2) % 3
        lever.append(n[a] * force[b] - n[b] * force[a])
    return force, lever, moment


def three_parts(value):
    high = value.astype(jnp.bfloat16)
    rest = value - high.astype(jnp.float32)
    middle = rest.astype(jnp.bfloat16)
    low = (rest - middle.astype(jnp.float32)).astype(jnp.bfloat16)
    return jnp.concatenate([high, middle], axis=0), low


def fetch(copies, sems):
    started = [
        pltpu.make_async_copy(source, target, sems.at[i])
        for i, (source, target) in enumerate(copies)
    ]
    for copy in started:
        copy.start()
    return started


def one_hot(index_tile, width):
    rows = index_tile.shape[0]
    padded = index_tile
    if rows < LANES:
        padded = jnp.concatenate(
            [index_tile, jnp.zeros((LANES - rows, LANES), index_tile.dtype)], axis=0
        )
    turned = jnp.transpose(padded)
    lane = lax.broadcasted_iota(jnp.int32, (LANES, width), 1).astype(jnp.float32)

    def make(row):
        return jnp.where(turned[:, row : row + 1] == lane, 1.0, 0.0).astype(jnp.bfloat16)

    return make


def send_setup(
    plan, own_h, slot_h, kind_h, normal_h, radii_h, rhs_h,
    message, mine, own, slot, kind, normal, radii, rhs, stack, sems,
):
    first = plan.near // LANES
    lanes = pl.ds(first * LANES, plan.contacts - first * LANES)
    for copy in fetch(
        [
            (own_h, own),
            (slot_h, slot),
            (kind_h, kind),
            (normal_h, normal),
            (radii_h.at[0, 0, 0, :, lanes], radii),
            (rhs_h, rhs),
        ],
        sems,
    ):
        copy.wait()
    for t in range(first, plan.tiles):
        at = (t - first) * 8
        lanes = slice(at * 16, at * 16 + LANES)
        stack[at : at + 1, :] = own[t : t + 1, :].astype(jnp.float32)
        stack[at + 1 : at + 2, :] = jnp.bitwise_and(slot[t : t + 1, :], plan.rim - 1).astype(
            jnp.float32
        )
        stack[at + 2 : at + 3, :] = kind[t : t + 1, :].astype(jnp.float32)
        stack[at + 3 : at + 6, :] = row_of(normal, t, plan.tiles, 3)
        stack[at + 6 : at + 8, :] = radii[:, lanes]
    lane = lax.broadcasted_iota(jnp.int32, (8, LANES), 1)
    row = lax.broadcasted_iota(jnp.int32, (8, LANES), 0)
    where = plan.neighbours()
    ghosts = [row_of(rhs, t, plan.grain_tiles, FIELDS) for t in range(plan.rim_tiles)]
    for e, (_, groups) in enumerate(plan.sides):
        chunk = jnp.where(row == 2, float(plan.types), 0.0)
        for j, k in enumerate(groups):
            place = plan.near + k * plan.group
            t, inside = place // LANES, place % LANES
            tile = stack[(t - first) * 8 : (t - first) * 8 + 8, :]
            turn = (j * plan.group - inside) % LANES
            if turn:
                tile = pltpu.roll(tile, turn, 1)
            here = (lane >= j * plan.group) & (lane < (j + 1) * plan.group)
            chunk = jnp.where(here, tile, chunk)
        mine[e * 8 : e * 8 + 8, :] = chunk
        packed = jnp.where(lane < plan.half, chunk, pltpu.roll(pltpu.roll(chunk, 4, 0), plan.half, 1))
        for t in range(plan.rim_tiles):
            message[where[e], 8 * t : 8 * t + FIELDS, :] = ghosts[t]
            message[where[e], 8 * t + FIELDS : 8 * t + 8, :] = packed[2 * t : 2 * t + 2, :]


def near_part(plan, field, diag, own, slot, table, image, seen, push, left, hot):
    rows = plan.near_tiles
    tiles = [field[:, s * LANES : (s + 1) * LANES] for s in range(plan.grain_tiles)]
    for side, index in enumerate((own, slot)):
        for t in range(rows):
            at = (side * rows + t) * 8
            seen[at : at + 8, :] = lane_gather(tiles, spread(index, t))
    first = [row_of(seen, c, 8, rows) for c in range(FIELDS)]
    second = [row_of(seen, rows * 8 + c, 8, rows) for c in range(FIELDS)]
    consts = [table[k, 0:rows, :] for k in range(9)]
    force, lever, moment = response(first, second, consts)
    for c in range(3):
        push[pl.ds(c, rows, stride=8), :] = force[c]
        push[pl.ds(3 + c, rows, stride=8), :] = consts[3] * lever[c] + moment[c]
        push[pl.ds(rows * 8 + c, rows, stride=8), :] = -force[c]
        push[pl.ds(rows * 8 + 3 + c, rows, stride=8), :] = consts[4] * lever[c] - moment[c]
    zero = jnp.zeros((2 * rows, LANES), jnp.float32)
    for c in range(FIELDS, 8):
        push[pl.ds(c, 2 * rows, stride=8), :] = zero
    parts = plan.grains // plan.rim
    grain = lax.broadcasted_iota(jnp.int32, (plan.rim, LANES), 0)
    for side, index in enumerate((own, slot)):
        for t in range(rows):
            at = side * rows + t
            value = push[at * 8 : at * 8 + 8, :]
            part = lax.div(spread(index, t), plan.rim)
            lanes = slice(at * LANES, (at + 1) * LANES)
            lows = []
            for q in range(parts):
                pair, low = three_parts(jnp.where(part == q, value, 0.0))
                left[q * 16 : q * 16 + 16, lanes] = pair
                lows.append(low)
            for q in range(0, parts, 2):
                left[parts * 16 + q * 8 : parts * 16 + q * 8 + 16, lanes] = jnp.concatenate(
                    lows[q : q + 2], axis=0
                )
            low = jnp.bitwise_and(index[t : t + 1, :], plan.rim - 1)
            hot[:, lanes] = jnp.where(grain == low, 1.0, 0.0).astype(jnp.bfloat16)
    total = lax.dot_general(
        left[...], hot[...], (((1,), (1,)), ((), ())), preferred_element_type=jnp.float32
    )
    for q in range(parts):
        lanes = slice(q * plan.rim, (q + 1) * plan.rim)
        at = parts * 16 + q * 8
        force = total[at : at + 8, :] + total[q * 16 + 8 : q * 16 + 16, :]
        force = force + total[q * 16 : q * 16 + 8, :]
        image[:, lanes] = diag[:, lanes] * field[:, lanes] - force


def near_first(
    plan, stiff_h, own_h, slot_h, kind_h, normal_h, radii_h, rhs_h, diag_h,
    image, table, field, diag, own, slot, stiff, kind, radii, rhs, ground, seen, push, left, hot, sems,
):
    rows = plan.near_tiles
    copies = fetch(
        [
            (stiff_h, stiff),
            (own_h, own),
            (slot_h, slot),
            (kind_h, kind),
            (radii_h.at[0, 0, 0], radii),
            (rhs_h, rhs),
            (diag_h, ground),
        ]
        + [(normal_h.at[pl.ds(c * plan.tiles, plan.tiles), :], table.at[c]) for c in range(3)],
        sems,
    )
    for copy in copies:
        copy.wait()
    for source, target in ((rhs, field), (ground, diag)):
        target[FIELDS:, :] = jnp.zeros((8 - FIELDS, plan.grains), jnp.float32)
        for t in range(plan.grain_tiles):
            target[0:FIELDS, t * LANES : (t + 1) * LANES] = row_of(
                source, t, plan.grain_tiles, FIELDS
            )
    for t in range(rows):
        lanes = slice(t * LANES, (t + 1) * LANES)
        for c in range(2):
            table[3 + c, t : t + 1, :] = radii[c : c + 1, lanes]
    lane = lax.broadcasted_iota(jnp.int32, (rows, LANES), 1)
    line = lax.broadcasted_iota(jnp.int32, (rows, LANES), 0)
    valid = line * LANES + lane < plan.near
    for k, value in enumerate(coefficients(stiff, kind[0:rows, :], plan.types, valid)):
        table[5 + k, 0:rows, :] = value
    near_part(plan, field, diag, own, slot, table, image, seen, push, left, hot)


def far_forces(plan, local, there, table, hot, push, left):
    rows = plan.far
    first = [row_of(local, c, 8, rows) for c in range(FIELDS)]
    second = [row_of(there, c, 8, rows) for c in range(FIELDS)]
    consts = [table[k, 0:rows, :] for k in range(9)]
    force, lever, moment = response(first, second, consts)
    for c in range(3):
        push[pl.ds(c, rows, stride=8), :] = force[c]
        push[pl.ds(3 + c, rows, stride=8), :] = consts[3] * lever[c] + moment[c]
    zero = jnp.zeros((rows, LANES), jnp.float32)
    for c in range(FIELDS, 8):
        push[pl.ds(c, rows, stride=8), :] = zero
    for e in range(rows):
        lanes = slice(e * LANES, (e + 1) * LANES)
        pair, low = three_parts(push[e * 8 : e * 8 + 8, :])
        left[0:16, lanes] = pair
        left[16:32, lanes] = jnp.concatenate([low, jnp.zeros_like(low)], axis=0)
    total = jnp.dot(left[...], hot[...], preferred_element_type=jnp.float32)
    return total[0:8, :] + (total[8:16, :] + total[16:24, :])


def send_rim(plan, field, index, sums, message, local):
    row = lax.broadcasted_iota(jnp.int32, (8, LANES), 0)
    base = jnp.where(row == FIELDS, sums[0], jnp.where(row == FIELDS + 1, sums[1], 0.0))
    message[...] = jnp.broadcast_to(base[None], message.shape)
    tiles = [field[:, t * LANES : (t + 1) * LANES] for t in range(plan.rim_tiles)]
    where = plan.neighbours()
    for e in range(plan.far):
        tile = lane_gather(tiles, spread(index, e))
        local[e * 8 : e * 8 + 8, :] = tile
        message[where[e], :, :] = jnp.where(row < FIELDS, pltpu.roll(tile, plan.half, 1), base)


def partial_sum(left, right):
    product = left * right
    total = product[:, 0:LANES]
    for t in range(1, product.shape[1] // LANES):
        total = total + product[:, t * LANES : (t + 1) * LANES]
    return jnp.sum(total, axis=0, keepdims=True)


def full_sum(received, row):
    return jnp.sum(jnp.sum(received[:, row, :], axis=0, keepdims=True), axis=1, keepdims=True)


def far_first(
    plan, stiff, received, mine, field, image,
    w, message, table, index, hot, local, merged, there, push, left,
):
    lane8 = lax.broadcasted_iota(jnp.int32, (8, LANES), 1)
    where = plan.neighbours()
    rows = plan.far
    for e in range(rows):
        own = pltpu.roll(mine[e * 8 : e * 8 + 8, :], plan.half, 1)
        packed = jnp.concatenate(
            [
                received[where[e], 8 * t + FIELDS : 8 * t + 8, :]
                for t in range(plan.rim_tiles)
            ],
            axis=0,
        )
        chunk = jnp.concatenate([packed, pltpu.roll(packed, plan.half, 1)], axis=0)
        merged[e * 8 : e * 8 + 8, :] = jnp.where(lane8 < plan.half, chunk, own)
    mirror = lax.broadcasted_iota(jnp.int32, (rows, LANES), 1) < plan.half
    row = [row_of(merged, r, 8, rows) for r in range(8)]
    for c in range(3):
        table[c, 0:rows, :] = jnp.where(mirror, -row[3 + c], row[3 + c])
    table[3, 0:rows, :] = jnp.where(mirror, row[7], row[6])
    table[4, 0:rows, :] = jnp.where(mirror, row[6], row[7])
    for k, value in enumerate(coefficients(stiff, row[2], plan.types)):
        table[5 + k, 0:rows, :] = value
    here = jnp.where(mirror, row[1], row[0])
    away = jnp.where(mirror, row[0], row[1]).astype(jnp.int32)
    index[0:rows, :] = here.astype(jnp.int32)
    make = one_hot(here, plan.rim)
    tiles = [field[:, t * LANES : (t + 1) * LANES] for t in range(plan.rim_tiles)]
    for e in range(rows):
        hot[e * LANES : (e + 1) * LANES, :] = make(e)
        local[e * 8 : e * 8 + 8, :] = lane_gather(tiles, spread(index, e))
        ghosts = [received[where[e], 8 * t : 8 * t + 8, :] for t in range(plan.rim_tiles)]
        there[e * 8 : e * 8 + 8, :] = lane_gather(
            ghosts, jnp.broadcast_to(away[e : e + 1, :], (8, LANES))
        )
    force = far_forces(plan, local, there, table, hot, push, left)
    w[...] = image[...]
    w[:, 0 : plan.rim] = image[:, 0 : plan.rim] - force
    r = field[...]
    sums = (partial_sum(r, r), partial_sum(w[...], r))
    send_rim(plan, w, index, sums, message, local)


def far_step(plan, number, *refs):
    refs = list(refs)

    def take(count):
        return [refs.pop(0) for _ in range(count)]

    received, image, table, index, hot, local, r, w = take(8)
    if number:
        p, s, z, x, past = take(5)
    last = number == ITERS - 2
    r_new, p_new, s_new, x_new, w_new, past_new = take(6)
    if not last:
        z_new, message, local_new = take(3)
    else:
        (message,) = take(1)
    there, push, left = take(3)

    where = plan.neighbours()
    for e in range(plan.far):
        there[e * 8 : e * 8 + 8, :] = received[where[e], :, :]
    gamma = full_sum(received, FIELDS)
    delta = full_sum(received, FIELDS + 1)
    force = far_forces(plan, local, there, table, hot, push, left)
    q = jnp.concatenate(
        [image[:, 0 : plan.rim] - force, image[:, plan.rim :]], axis=1
    )
    if number:
        beta = gamma / past[0:1, 0:1]
        alpha = gamma / (delta - beta * gamma / past[1:2, 0:1])
        z_now = q + beta * z[...]
        s_now = w[...] + beta * s[...]
        p_now = r[...] + beta * p[...]
        x_new[...] = x[...] + alpha * p_now
    else:
        alpha = gamma / delta
        z_now = q
        s_now = w[...]
        p_now = r[...]
        x_new[...] = alpha * p_now
    r_now = r[...] - alpha * s_now
    w_now = w[...] - alpha * z_now
    r_new[...] = r_now
    w_new[...] = w_now
    p_new[...] = p_now
    s_new[...] = s_now
    past_new[0:1, :] = jnp.broadcast_to(gamma, (1, LANES))
    past_new[1:2, :] = jnp.broadcast_to(alpha, (1, LANES))
    sums = (partial_sum(r_now, r_now), partial_sum(w_now, r_now))
    if not last:
        z_new[...] = z_now
        send_rim(plan, w_new, index, sums, message, local_new)
    else:
        base = jnp.concatenate(sums, axis=0)
        message[...] = jnp.broadcast_to(base[None], message.shape)


def finish(plan, received, r, w, p, s, x, past, x_out, r_out, x_last, r_last, sems):
    gamma = full_sum(received, 0)
    delta = full_sum(received, 1)
    beta = gamma / past[0:1, 0:1]
    alpha = gamma / (delta - beta * gamma / past[1:2, 0:1])
    for t in range(plan.grain_tiles):
        here = slice(0, FIELDS), slice(t * LANES, (t + 1) * LANES)
        there = pl.ds(t, FIELDS, stride=plan.grain_tiles), slice(None)
        x_last[there] = x[here] + alpha * (r[here] + beta * p[here])
        r_last[there] = r[here] - alpha * (w[here] + beta * s[here])
    for copy in fetch([(x_last, x_out), (r_last, r_out)], sems):
        copy.wait()


def shards(
    mesh,
    right_side,
    grain_diag,
    stiffness,
    contact_own,
    contact_slot,
    contact_type,
    contact_normal,
    contact_radii,
):
    plan = Plan(mesh, right_side.shape[-1], contact_own.shape[-1], stiffness.shape[1])
    own = contact_own.reshape(plan.tiles, LANES)
    slot = contact_slot.reshape(plan.tiles, LANES)
    kind = contact_type.reshape(plan.tiles, LANES)
    normal = contact_normal.reshape(3 * plan.tiles, LANES)
    lines = (FIELDS * plan.grain_tiles, LANES)
    rhs = right_side.reshape(lines)
    ground = grain_diag.reshape(lines)
    f32, bf16, i32 = jnp.float32, jnp.bfloat16, jnp.int32
    vmem, hbm, dma = pltpu.MemorySpace.VMEM, pltpu.MemorySpace.HBM, pltpu.SemaphoreType.DMA
    wide = (8, plan.grains)
    far = (plan.far * 8, LANES)
    far_table = (9, -(-plan.far // 8) * 8, LANES)
    near_table = (9, plan.tiles, LANES)
    table = (plan.tiles, LANES)
    near_rows = 2 * plan.near_tiles
    parts = plan.grains // plan.rim
    rest = plan.contacts - plan.near // LANES * LANES

    def call(body, outs, scratch, *args, raw=False, end=False):
        space = hbm if raw else vmem
        args = [pltpu.with_memory_space_constraint(x, space) for x in args]
        return pl.pallas_call(
            functools.partial(body, plan),
            out_shape=[(hbm if end else vmem)(dims, dtype) for dims, dtype in outs],
            in_specs=[pl.BlockSpec(memory_space=space)] * len(args),
            out_specs=[pl.BlockSpec(memory_space=hbm if end else vmem)] * len(outs),
            scratch_shapes=scratch,
            compiler_params=pltpu.CompilerParams(vmem_limit_bytes=16 * 2**20),
        )(*args)

    def exchange(message):
        return lax.all_to_all(message, AXES, 0, 0)

    tile = (plan.devices, 8, LANES)
    near_scratch = [
        vmem((near_rows * 8, LANES), f32),
        vmem((near_rows * 8, LANES), f32),
        vmem((parts * 24, near_rows * LANES), bf16),
        vmem((plan.rim, near_rows * LANES), bf16),
    ]
    far_scratch = [vmem(far, f32), vmem(far, f32), vmem((32, plan.far * LANES), bf16)]

    message, mine = call(
        send_setup,
        [((plan.devices, 8 * plan.rim_tiles, LANES), f32), (far, f32)],
        [
            vmem(table, i32),
            vmem(table, i32),
            vmem(table, i32),
            vmem(normal.shape, f32),
            vmem((2, rest), f32),
            vmem(lines, f32),
            vmem((rest // LANES * 8, LANES), f32),
            dma((6,)),
        ],
        own, slot, kind, normal, contact_radii, rhs,
        raw=True,
    )
    received = exchange(message)
    image, near_const, field, diag, own, slot, stiff = call(
        near_first,
        [
            (wide, f32),
            (near_table, f32),
            (wide, f32),
            (wide, f32),
            (table, i32),
            (table, i32),
            (stiffness.shape, f32),
        ],
        [vmem(table, i32), vmem((2, plan.contacts), f32), vmem(lines, f32), vmem(lines, f32)]
        + near_scratch
        + [dma((10,))],
        stiffness, own, slot, kind, normal, contact_radii, rhs, ground,
        raw=True,
    )
    w, message, far_const, index, far_hot, local = call(
        far_first,
        [
            (wide, f32),
            (tile, f32),
            (far_table, f32),
            (far_table[1:], i32),
            ((plan.far * LANES, plan.rim), bf16),
            (far, f32),
        ],
        [vmem(far, f32)] + far_scratch,
        stiff, received, mine, field, image,
    )
    r = field
    state = ()
    for number in range(ITERS - 1):
        received = exchange(message)
        (image,) = call(
            near_part,
            [(wide, f32)],
            near_scratch,
            w, diag, own, slot, near_const,
        )
        last = number == ITERS - 2
        outs = [(wide, f32)] * 5 + [((8, LANES), f32)]
        if last:
            outs = outs + [((plan.devices, 2, LANES), f32)]
        else:
            outs = outs + [(wide, f32), (tile, f32), (far, f32)]
        made = call(
            lambda plan, *refs, number=number: far_step(plan, number, *refs),
            outs,
            far_scratch,
            received, image, far_const, index, far_hot, local, r, w, *state,
        )
        r, p, s, x, w, past = made[:6]
        if last:
            message = made[6]
        else:
            z, message, local = made[6:]
            state = (p, s, z, x, past)
    received = exchange(message)
    solution_field, residual = call(
        finish,
        [(lines, f32)] * 2,
        [vmem(lines, f32), vmem(lines, f32), dma((2,))],
        received, r, w, p, s, x, past,
        end=True,
    )
    return (solution_field.reshape(right_side.shape), residual.reshape(right_side.shape))


def solution(mesh):
    vector = P("gx", "gy", "gz", None)
    matrix = P("gx", "gy", "gz", None, None)
    return jax.shard_map(
        functools.partial(shards, mesh),
        mesh=mesh,
        in_specs=(matrix, matrix, P(), vector, vector, vector, matrix, matrix),
        out_specs=(matrix, matrix),
        check_vma=False,
    )
```

profile of v0, /device:TPU:0, one launch (start us, length us, event | category | flops | bytes accessed | tf_op | source)
XLA Modules:
  0.0 67.1 jit_solution(6375789989854280636)
XLA Ops:
  0.6 1.8 %shard_map.96 = (f32[32,16,128]{2,1,0:T(8,128)}, f32[136,128]{1,0:T(8,128)S(1)}) custom-call(s32[24,128]{1,0:T(8,128)} %bitcast.12, s32[24,128]{1,0:T(8,128)} %bitcast.14, s32[24,128]{1,0:T(8,128)} %bitcast.16, f32[72,128]{1,0:T(8,128)} %bitcast.8, f32[1,1,1,2,3072]{4,3,2,1,0:T(2,128)} %radii_h.3, f32[48,128]{1,0:T(8,128)} %bitcast.10), custom_call_target="tpu_custom_call" | custom-call | tf_op jit(solution)/shard_map/pallas_call | solution.py:467
  2.4 7.3 %all-to-all-start = ((f32[32,16,128]{2,1,0:T(8,128)}), f32[32,16,128]{2,1,0:T(8,128)S(1)}, u32[]{:S(2)}, u32[]{:S(2)}) async-start(f32[32,16,128]{2,1,0:T(8,128)} %get-tuple-element.45), calls=%async_computation | async-start | bytes 524288 | tf_op jit(solution)/shard_map/all_to_all | solution.py:477
  9.7 2.8 %shard_map.95 = (f32[8,1024]{1,0:T(8,128)S(1)}, f32[9,24,128]{2,1,0:T(8,128)S(1)}, f32[8,1024]{1,0:T(8,128)S(1)}, f32[8,1024]{1,0:T(8,128)S(1)}, s32[24,128]{1,0...) custom-call(f32[4,4]{1,0:T(4,128)} %stiff_h.1, s32[24,128]{1,0:T(8,128)} %bitcast.13, s32[24,128]{1,0:T(8,128)} %bitcast.15, ...), custom_call_target="tpu_custom_call" | custom-call | tf_op jit(solution)/shard_map/pallas_call | solution.py:467
  12.5 7.8 %all-to-all-done.received = f32[32,16,128]{2,1,0:T(8,128)S(1)} async-done(((f32[32,16,128]{2,1,0:T(8,128)}), f32[32,16,128]{2,1,0:T(8,128)S(1)}, u32[]{:S(2)}, u32[]{:S(2)}) %all-to-all-start) | async-done | bytes 262176 | tf_op jit(solution)/shard_map/all_to_all | solution.py:477
  20.3 1.8 %shard_map.97 = (f32[8,1024]{1,0:T(8,128)S(1)}, f32[32,8,128]{2,1,0:T(8,128)}, f32[9,24,128]{2,1,0:T(8,128)S(1)}, s32[24,128]{1,0:T(8,128)S(1)}, bf16[2176,256]{1,0:T(8,128)(2,1)S(1)}, /*index=5*/f32[136,128]{1,0:T(8,128)S(1)}) custom-call(f32[4,4]{1,0:T(4,128)S(1)} %get-tuple-element.44.stiff, f32[32,16,128]{2,1,0:T(8,128)S(1)} %all-to-all-done.received, ...), custom_call_target="tpu_custom_call" | custom-call | tf_op jit(solution)/shard_map/pallas_call | solution.py:467
  22.1 2.6 %all-to-all-start.1 = ((f32[32,8,128]{2,1,0:T(8,128)}), f32[32,8,128]{2,1,0:T(8,128)S(1)}, u32[]{:S(2)}, u32[]{:S(2)}) async-start(f32[32,8,128]{2,1,0:T(8,128)} %get-tuple-element.49), calls=%async_computation.1 | async-start | bytes 262144 | tf_op jit(solution)/shard_map/all_to_all | solution.py:477
  24.7 1.8 %shard_map.98.refs_1_ = f32[8,1024]{1,0:T(8,128)S(1)} custom-call(f32[8,1024]{1,0:T(8,128)S(1)} %get-tuple-element.50.field.refs_7_, f32[8,1024]{1,0:T(8,128)S(1)} %get-tuple-element.51.diag, s32[24,128]{1,0:T(8,128)S(1)} %get-tuple-element.52.own, s32[24,128]{1,0:T(8,128)S(1)} %get-tuple-element.53.slot, f32[9,24,128]{2,1,0:T(8,128)S(1)} %get-tuple-element.54.table), custom_call_target="tpu_custom_call" | custom-call | tf_op jit(solution)/shard_map/pallas_call | solution.py:467
  26.6 6.4 %all-to-all-done.1.refs_0_ = f32[32,8,128]{2,1,0:T(8,128)S(1)} async-done(((f32[32,8,128]{2,1,0:T(8,128)}), f32[32,8,128]{2,1,0:T(8,128)S(1)}, u32[]{:S(2)}, u32[]{:S(2)}) %all-to-all-start.1) | async-done | bytes 131104 | tf_op jit(solution)/shard_map/all_to_all | solution.py:477
  32.9 1.2 %shard_map.99 = (f32[8,1024]{1,0:T(8,128)S(1)}, f32[8,1024]{1,0:T(8,128)S(1)}, f32[8,1024]{1,0:T(8,128)S(1)}, f32[8,1024]{1,0:T(8,128)S(1)}, f32[8,1024]{1,0:T(8...) custom-call(f32[32,8,128]{2,1,0:T(8,128)S(1)} %all-to-all-done.1.refs_, ...), custom_call_target="tpu_custom_call" | custom-call | tf_op jit(solution)/shard_map/pallas_call | solution.py:467
  34.2 2.6 %all-to-all-start.2 = ((f32[32,8,128]{2,1,0:T(8,128)}), f32[32,8,128]{2,1,0:T(8,128)S(1)}, u32[]{:S(2)}, u32[]{:S(2)}) async-start(f32[32,8,128]{2,1,0:T(8,128)} %get-tuple-element.59), calls=%async_computation.2 | async-start | bytes 262144 | tf_op jit(solution)/shard_map/all_to_all | solution.py:477
  36.7 1.8 %shard_map.100.refs_1_ = f32[8,1024]{1,0:T(8,128)S(1)} custom-call(f32[8,1024]{1,0:T(8,128)S(1)} %get-tuple-element.60.field.refs_7_, f32[8,1024]{1,0:T(8,128)S(1)} %get-tuple-element.51.diag, s32[24,128]{1,0:T(8,128)S(1)} %get-tuple-element.52.own, s32[24,128]{1,0:T(8,128)S(1)} %get-tuple-element.53.slot, f32[9,24,128]{2,1,0:T(8,128)S(1)} %get-tuple-element.54.table), custom_call_target="tpu_custom_call" | custom-call | tf_op jit(solution)/shard_map/pallas_call | solution.py:467
  38.6 6.4 %all-to-all-done.2.refs_0_ = f32[32,8,128]{2,1,0:T(8,128)S(1)} async-done(((f32[32,8,128]{2,1,0:T(8,128)}), f32[32,8,128]{2,1,0:T(8,128)S(1)}, u32[]{:S(2)}, u32[]{:S(2)}) %all-to-all-start.2) | async-done | bytes 131104 | tf_op jit(solution)/shard_map/all_to_all | solution.py:477
  45.0 1.2 %shard_map.101 = (f32[8,1024]{1,0:T(8,128)S(1)}, f32[8,1024]{1,0:T(8,128)S(1)}, f32[8,1024]{1,0:T(8,128)S(1)}, f32[8,1024]{1,0:T(8,128)S(1)}, f32[8,1024]{1,0:T(...) custom-call(f32[32,8,128]{2,1,0:T(8,128)S(1)} %all-to-all-done.2.refs, ...), custom_call_target="tpu_custom_call" | custom-call | tf_op jit(solution)/shard_map/pallas_call | solution.py:467
  46.2 2.6 %all-to-all-start.3 = ((f32[32,8,128]{2,1,0:T(8,128)}), f32[32,8,128]{2,1,0:T(8,128)S(1)}, u32[]{:S(2)}, u32[]{:S(2)}) async-start(f32[32,8,128]{2,1,0:T(8,128)} %get-tuple-element.68), calls=%async_computation.3 | async-start | bytes 262144 | tf_op jit(solution)/shard_map/all_to_all | solution.py:477
  48.8 1.8 %shard_map.102.refs_1_ = f32[8,1024]{1,0:T(8,128)S(1)} custom-call(f32[8,1024]{1,0:T(8,128)S(1)} %get-tuple-element.69.field.refs_7_, f32[8,1024]{1,0:T(8,128)S(1)} %get-tuple-element.51.diag, s32[24,128]{1,0:T(8,128)S(1)} %get-tuple-element.52.own, s32[24,128]{1,0:T(8,128)S(1)} %get-tuple-element.53.slot, f32[9,24,128]{2,1,0:T(8,128)S(1)} %get-tuple-element.54.table), custom_call_target="tpu_custom_call" | custom-call | tf_op jit(solution)/shard_map/pallas_call | solution.py:467
  50.6 6.4 %all-to-all-done.3.refs_0_ = f32[32,8,128]{2,1,0:T(8,128)S(1)} async-done(((f32[32,8,128]{2,1,0:T(8,128)}), f32[32,8,128]{2,1,0:T(8,128)S(1)}, u32[]{:S(2)}, u32[]{:S(2)}) %all-to-all-start.3) | async-done | bytes 131104 | tf_op jit(solution)/shard_map/all_to_all | solution.py:477
  57.0 0.4 shard_map.103
  57.4 8.9 %all_to_all.25.received = f32[32,2,128]{2,1,0:T(2,128)S(1)} all-to-all(f32[32,2,128]{2,1,0:T(2,128)S(1)} %get-tuple-element.77), channel_id=1, replica_groups=mesh['gx'=4,'gy'=2,'gz'=4] {'gx','gy','gz'}, dimensions={0} | all-to-all | bytes 65536 | tf_op jit(solution)/shard_map/all_to_all | solution.py:477
  66.3 0.8 %shard_map.104 = (f32[48,128]{1,0:T(8,128)}, f32[48,128]{1,0:T(8,128)}) custom-call(f32[32,2,128]{2,1,0:T(2,128)S(1)} %all_to_all.25.received, f32[8,1024]{1,0:T(8,128)S(1)} %get-tuple-element.78.r, f32[8,1024]{1,0:T(8,128)S(1)} %get-tuple-element.79.w, f32[8,1024]{1,0:T(8,128)S(1)} %get-tuple-element.80.p, f32[8,1024]{1,0:T(8,128)S(1)} %get-tuple-element.81.s, ...), custom_call_target="tpu_custom_call" | custom-call | tf_op jit(solution)/shard_map/pallas_call | solution.py:467
Async XLA Ops:
  2.4 17.9 %all-to-all-start = ((f32[32,16,128]{2,1,0:T(8,128)}), f32[32,16,128]{2,1,0:T(8,128)S(1)}, u32[]{:S(2)}, u32[]{:S(2)}) async-start(f32[32,16,128]{2,1,0:T(8,128)} %get-tuple-element.45), calls=%async_computation | async-start | bytes 524288 | tf_op jit(solution)/shard_map/all_to_all | solution.py:477
  22.1 10.8 %all-to-all-start.1 = ((f32[32,8,128]{2,1,0:T(8,128)}), f32[32,8,128]{2,1,0:T(8,128)S(1)}, u32[]{:S(2)}, u32[]{:S(2)}) async-start(f32[32,8,128]{2,1,0:T(8,128)} %get-tuple-element.49), calls=%async_computation.1 | async-start | bytes 262144 | tf_op jit(solution)/shard_map/all_to_all | solution.py:477
  34.2 10.8 %all-to-all-start.2 = ((f32[32,8,128]{2,1,0:T(8,128)}), f32[32,8,128]{2,1,0:T(8,128)S(1)}, u32[]{:S(2)}, u32[]{:S(2)}) async-start(f32[32,8,128]{2,1,0:T(8,128)} %get-tuple-element.59), calls=%async_computation.2 | async-start | bytes 262144 | tf_op jit(solution)/shard_map/all_to_all | solution.py:477
  46.2 10.8 %all-to-all-start.3 = ((f32[32,8,128]{2,1,0:T(8,128)}), f32[32,8,128]{2,1,0:T(8,128)S(1)}, u32[]{:S(2)}, u32[]{:S(2)}) async-start(f32[32,8,128]{2,1,0:T(8,128)} %get-tuple-element.68), calls=%async_computation.3 | async-start | bytes 262144 | tf_op jit(solution)/shard_map/all_to_all | solution.py:477
where the time goes:
time: 67.7 us; the launch traced here: 67.1 us
  waiting for transfers between devices  26.9 us (40%)
  Pallas kernels  15.6 us (23%)
  starting transfers between devices  15 us (22%)
  blocking collectives  8.95 us (13%)
  between operations  0.71 us (1%)
    all_to_all x4, waiting for transfers between devices, exchange(): return lax.all_to_all(message, AXES, 0, 0)  26.9 us
    pallas_call x10, Pallas kernels, call(): pl.pallas_call(functools.partial(body, plan), out_shape=[(hbm if end else...  15.6 us
    all_to_all x4, starting transfers between devices, exchange(): return lax.all_to_all(message, AXES, 0, 0)  15 us
    all_to_all x1, blocking collectives, exchange(): return lax.all_to_all(message, AXES, 0, 0)  8.95 us
  transfers between devices with their start and end apart: 4, of which 4 were waited for; matrix products, arithmetic and copies ran while one was open for 0% of the time, Pallas kernels for 12%

commit v1 on v0

--- a/solution.py
+++ b/solution.py
@@ -19,11 +19,14 @@
         self.devices = self.counts[0] * self.counts[1] * self.counts[2]
         self.grains = grains
         self.rim = grains // 4
+        self.rim_bits = self.rim.bit_length() - 1
         self.group = grains // 32
         self.contacts = contacts
         self.types = types
         self.near = contacts - 26 * self.group
         self.near_tiles = -(-self.near // LANES)
+        middle = self.near_tiles // 16 * 8
+        self.near_groups = [(0, middle), (middle, self.near_tiles)] if middle else [(0, self.near_tiles)]
         self.tiles = contacts // LANES
         self.grain_tiles = grains // LANES
         self.rim_tiles = self.rim // LANES
@@ -100,11 +103,14 @@
 
 
 def three_parts(value):
-    high = value.astype(jnp.bfloat16)
-    rest = value - high.astype(jnp.float32)
-    middle = rest.astype(jnp.bfloat16)
-    low = (rest - middle.astype(jnp.float32)).astype(jnp.bfloat16)
-    return jnp.concatenate([high, middle], axis=0), low
+    high = value.astype(jnp.bfloat16).astype(jnp.float32)
+    rest = value - high
+    middle = rest.astype(jnp.bfloat16).astype(jnp.float32)
+    return high, middle, rest - middle
+
+
+def stacked(upper, lower):
+    return jnp.concatenate([upper, lower], axis=0).astype(jnp.bfloat16)
 
 
 def fetch(copies, sems):
@@ -183,47 +189,50 @@
             message[where[e], 8 * t + FIELDS : 8 * t + 8, :] = packed[2 * t : 2 * t + 2, :]
 
 
-def near_part(plan, field, diag, own, slot, table, image, seen, push, left, hot):
-    rows = plan.near_tiles
+def near_part(plan, field, diag, own, slot, table, hot, image, seen, push, left):
     tiles = [field[:, s * LANES : (s + 1) * LANES] for s in range(plan.grain_tiles)]
-    for side, index in enumerate((own, slot)):
-        for t in range(rows):
-            at = (side * rows + t) * 8
-            seen[at : at + 8, :] = lane_gather(tiles, spread(index, t))
-    first = [row_of(seen, c, 8, rows) for c in range(FIELDS)]
-    second = [row_of(seen, rows * 8 + c, 8, rows) for c in range(FIELDS)]
-    consts = [table[k, 0:rows, :] for k in range(9)]
-    force, lever, moment = response(first, second, consts)
-    for c in range(3):
-        push[pl.ds(c, rows, stride=8), :] = force[c]
-        push[pl.ds(3 + c, rows, stride=8), :] = consts[3] * lever[c] + moment[c]
-        push[pl.ds(rows * 8 + c, rows, stride=8), :] = -force[c]
-        push[pl.ds(rows * 8 + 3 + c, rows, stride=8), :] = consts[4] * lever[c] - moment[c]
-    zero = jnp.zeros((2 * rows, LANES), jnp.float32)
-    for c in range(FIELDS, 8):
-        push[pl.ds(c, 2 * rows, stride=8), :] = zero
     parts = plan.grains // plan.rim
-    grain = lax.broadcasted_iota(jnp.int32, (plan.rim, LANES), 0)
-    for side, index in enumerate((own, slot)):
-        for t in range(rows):
-            at = side * rows + t
-            value = push[at * 8 : at * 8 + 8, :]
-            part = lax.div(spread(index, t), plan.rim)
-            lanes = slice(at * LANES, (at + 1) * LANES)
-            lows = []
-            for q in range(parts):
-                pair, low = three_parts(jnp.where(part == q, value, 0.0))
-                left[q * 16 : q * 16 + 16, lanes] = pair
-                lows.append(low)
-            for q in range(0, parts, 2):
-                left[parts * 16 + q * 8 : parts * 16 + q * 8 + 16, lanes] = jnp.concatenate(
-                    lows[q : q + 2], axis=0
-                )
-            low = jnp.bitwise_and(index[t : t + 1, :], plan.rim - 1)
-            hot[:, lanes] = jnp.where(grain == low, 1.0, 0.0).astype(jnp.bfloat16)
-    total = lax.dot_general(
-        left[...], hot[...], (((1,), (1,)), ((), ())), preferred_element_type=jnp.float32
-    )
+    total = None
+    for start, stop in plan.near_groups:
+        rows = stop - start
+        base = 2 * start
+        for side, index in enumerate((own, slot)):
+            for t in range(rows):
+                at = (base + side * rows + t) * 8
+                seen[at : at + 8, :] = lane_gather(tiles, spread(index, start + t))
+        one, two = base * 8, (base + rows) * 8
+        first = [row_of(seen, one + c, 8, rows) for c in range(FIELDS)]
+        second = [row_of(seen, two + c, 8, rows) for c in range(FIELDS)]
+        consts = [table[k, start:stop, :] for k in range(9)]
+        force, lever, moment = response(first, second, consts)
+        zero = jnp.zeros((rows, LANES), jnp.float32)
+        for c in range(3):
+            push[pl.ds(one + c, rows, stride=8), :] = force[c]
+            push[pl.ds(one + 3 + c, rows, stride=8), :] = consts[3] * lever[c] + moment[c]
+            push[pl.ds(two + c, rows, stride=8), :] = -force[c]
+            push[pl.ds(two + 3 + c, rows, stride=8), :] = consts[4] * lever[c] - moment[c]
+        for c in range(FIELDS, 8):
+            push[pl.ds(one + c, rows, stride=8), :] = zero
+            push[pl.ds(two + c, rows, stride=8), :] = zero
+        for side, index in enumerate((own, slot)):
+            for t in range(rows):
+                at = base + side * rows + t
+                lanes = slice(at * LANES, (at + 1) * LANES)
+                split = three_parts(push[at * 8 : at * 8 + 8, :])
+                part = lax.shift_right_logical(spread(index, start + t), plan.rim_bits)
+                lows = []
+                for q in range(parts):
+                    here = part == q
+                    high, middle, low = [jnp.where(here, x, 0.0) for x in split]
+                    left[q * 16 : q * 16 + 16, lanes] = stacked(high, middle)
+                    lows.append(low)
+                for q in range(0, parts, 2):
+                    left[parts * 16 + q * 8 : parts * 16 + q * 8 + 16, lanes] = stacked(
+                        lows[q], lows[q + 1]
+                    )
+        lanes = slice(base * LANES, (base + 2 * rows) * LANES)
+        sums = jnp.dot(left[:, lanes], hot[lanes, :], preferred_element_type=jnp.float32)
+        total = sums if total is None else total + sums
     for q in range(parts):
         lanes = slice(q * plan.rim, (q + 1) * plan.rim)
         at = parts * 16 + q * 8
@@ -234,7 +243,7 @@
 
 def near_first(
     plan, stiff_h, own_h, slot_h, kind_h, normal_h, radii_h, rhs_h, diag_h,
-    image, table, field, diag, own, slot, stiff, kind, radii, rhs, ground, seen, push, left, hot, sems,
+    image, table, field, diag, own, slot, stiff, hot, kind, radii, rhs, ground, seen, push, left, sems,
 ):
     rows = plan.near_tiles
     copies = fetch(
@@ -267,7 +276,14 @@
     valid = line * LANES + lane < plan.near
     for k, value in enumerate(coefficients(stiff, kind[0:rows, :], plan.types, valid)):
         table[5 + k, 0:rows, :] = value
-    near_part(plan, field, diag, own, slot, table, image, seen, push, left, hot)
+    for side, index in enumerate((own, slot)):
+        low = jnp.bitwise_and(index[...], plan.rim - 1).astype(jnp.float32)
+        make = one_hot(low, plan.rim)
+        for start, stop in plan.near_groups:
+            for t in range(start, stop):
+                at = (2 * start + side * (stop - start) + t - start) * LANES
+                hot[at : at + LANES, :] = make(t)
+    near_part(plan, field, diag, own, slot, table, hot, image, seen, push, left)
 
 
 def far_forces(plan, local, there, table, hot, push, left):
@@ -284,9 +300,9 @@
         push[pl.ds(c, rows, stride=8), :] = zero
     for e in range(rows):
         lanes = slice(e * LANES, (e + 1) * LANES)
-        pair, low = three_parts(push[e * 8 : e * 8 + 8, :])
-        left[0:16, lanes] = pair
-        left[16:32, lanes] = jnp.concatenate([low, jnp.zeros_like(low)], axis=0)
+        high, middle, low = three_parts(push[e * 8 : e * 8 + 8, :])
+        left[0:16, lanes] = stacked(high, middle)
+        left[16:32, lanes] = stacked(low, jnp.zeros_like(low))
     total = jnp.dot(left[...], hot[...], preferred_element_type=jnp.float32)
     return total[0:8, :] + (total[8:16, :] + total[16:24, :])
 
@@ -303,16 +319,38 @@
         message[where[e], :, :] = jnp.where(row < FIELDS, pltpu.roll(tile, plan.half, 1), base)
 
 
-def partial_sum(left, right):
-    product = left * right
-    total = product[:, 0:LANES]
-    for t in range(1, product.shape[1] // LANES):
-        total = total + product[:, t * LANES : (t + 1) * LANES]
-    return jnp.sum(total, axis=0, keepdims=True)
-
-
-def full_sum(received, row):
-    return jnp.sum(jnp.sum(received[:, row, :], axis=0, keepdims=True), axis=1, keepdims=True)
+def partial_sums(r, w, s=None, p=None):
+    def fold(product):
+        total = product[:, 0:LANES]
+        for t in range(1, product.shape[1] // LANES):
+            total = total + product[:, t * LANES : (t + 1) * LANES]
+        return total
+
+    def join(left, right):
+        low = lax.broadcasted_iota(jnp.int32, (8, LANES), 1) < LANES // 2
+        halves = [x + pltpu.roll(x, LANES // 2, 1) for x in (left, right)]
+        return jnp.sum(jnp.where(low, *halves), axis=0, keepdims=True)
+
+    if s is None:
+        zero = jnp.zeros((8, LANES), jnp.float32)
+        return join(fold(r * r), zero), join(fold(w * r), zero)
+    return join(fold(r * r), fold(r * s + p * w)), join(fold(w * r), fold(p * s))
+
+
+def full_sums(received, first):
+    low = lax.broadcasted_iota(jnp.int32, (1, LANES), 1) < LANES // 2
+    found = []
+    for row in (first, first + 1):
+        total = jnp.sum(received[:, row, :], axis=0, keepdims=True)
+        for half in (jnp.where(low, total, 0.0), jnp.where(low, 0.0, total)):
+            found.append(jnp.sum(half, axis=1, keepdims=True))
+    return found[0], found[2], found[1], found[3]
+
+
+def step_sizes(sums, past):
+    gamma, delta, mixed, energy = sums
+    beta = gamma / past[0:1, 0:1]
+    return gamma / (delta + beta * (mixed + beta * energy)), beta
 
 
 def far_first(
@@ -356,8 +394,7 @@
     force = far_forces(plan, local, there, table, hot, push, left)
     w[...] = image[...]
     w[:, 0 : plan.rim] = image[:, 0 : plan.rim] - force
-    r = field[...]
-    sums = (partial_sum(r, r), partial_sum(w[...], r))
+    sums = partial_sums(field[...], w[...])
     send_rim(plan, w, index, sums, message, local)
 
 
@@ -367,7 +404,7 @@
     def take(count):
         return [refs.pop(0) for _ in range(count)]
 
-    received, image, table, index, hot, local, r, w = take(8)
+    received, diag, own, slot, near_const, near_hot, table, index, hot, local, r, w = take(12)
     if number:
         p, s, z, x, past = take(5)
     last = number == ITERS - 2
@@ -376,26 +413,25 @@
         z_new, message, local_new = take(3)
     else:
         (message,) = take(1)
-    there, push, left = take(3)
+    image, near_seen, near_push, near_left, there, push, left = take(7)
+    near_part(plan, w, diag, own, slot, near_const, near_hot, image, near_seen, near_push, near_left)
 
     where = plan.neighbours()
     for e in range(plan.far):
         there[e * 8 : e * 8 + 8, :] = received[where[e], :, :]
-    gamma = full_sum(received, FIELDS)
-    delta = full_sum(received, FIELDS + 1)
+    sums = full_sums(received, FIELDS)
     force = far_forces(plan, local, there, table, hot, push, left)
     q = jnp.concatenate(
         [image[:, 0 : plan.rim] - force, image[:, plan.rim :]], axis=1
     )
     if number:
-        beta = gamma / past[0:1, 0:1]
-        alpha = gamma / (delta - beta * gamma / past[1:2, 0:1])
+        alpha, beta = step_sizes(sums, past)
         z_now = q + beta * z[...]
         s_now = w[...] + beta * s[...]
         p_now = r[...] + beta * p[...]
         x_new[...] = x[...] + alpha * p_now
     else:
-        alpha = gamma / delta
+        alpha = sums[0] / sums[1]
         z_now = q
         s_now = w[...]
         p_now = r[...]
@@ -406,9 +442,8 @@
     w_new[...] = w_now
     p_new[...] = p_now
     s_new[...] = s_now
-    past_new[0:1, :] = jnp.broadcast_to(gamma, (1, LANES))
-    past_new[1:2, :] = jnp.broadcast_to(alpha, (1, LANES))
-    sums = (partial_sum(r_now, r_now), partial_sum(w_now, r_now))
+    past_new[...] = jnp.broadcast_to(sums[0], past_new.shape)
+    sums = partial_sums(r_now, w_now, s_now, p_now)
     if not last:
         z_new[...] = z_now
         send_rim(plan, w_new, index, sums, message, local_new)
@@ -418,10 +453,7 @@
 
 
 def finish(plan, received, r, w, p, s, x, past, x_out, r_out, x_last, r_last, sems):
-    gamma = full_sum(received, 0)
-    delta = full_sum(received, 1)
-    beta = gamma / past[0:1, 0:1]
-    alpha = gamma / (delta - beta * gamma / past[1:2, 0:1])
+    alpha, beta = step_sizes(full_sums(received, 0), past)
     for t in range(plan.grain_tiles):
         here = slice(0, FIELDS), slice(t * LANES, (t + 1) * LANES)
         there = pl.ds(t, FIELDS, stride=plan.grain_tiles), slice(None)
@@ -481,7 +513,6 @@
         vmem((near_rows * 8, LANES), f32),
         vmem((near_rows * 8, LANES), f32),
         vmem((parts * 24, near_rows * LANES), bf16),
-        vmem((plan.rim, near_rows * LANES), bf16),
     ]
     far_scratch = [vmem(far, f32), vmem(far, f32), vmem((32, plan.far * LANES), bf16)]
 
@@ -502,7 +533,7 @@
         raw=True,
     )
     received = exchange(message)
-    image, near_const, field, diag, own, slot, stiff = call(
+    image, near_const, field, diag, own, slot, stiff, near_hot = call(
         near_first,
         [
             (wide, f32),
@@ -512,6 +543,7 @@
             (table, i32),
             (table, i32),
             (stiffness.shape, f32),
+            ((near_rows * LANES, plan.rim), bf16),
         ],
         [vmem(table, i32), vmem((2, plan.contacts), f32), vmem(lines, f32), vmem(lines, f32)]
         + near_scratch
@@ -536,12 +568,6 @@
     state = ()
     for number in range(ITERS - 1):
         received = exchange(message)
-        (image,) = call(
-            near_part,
-            [(wide, f32)],
-            near_scratch,
-            w, diag, own, slot, near_const,
-        )
         last = number == ITERS - 2
         outs = [(wide, f32)] * 5 + [((8, LANES), f32)]
         if last:
@@ -551,8 +577,8 @@
         made = call(
             lambda plan, *refs, number=number: far_step(plan, number, *refs),
             outs,
-            far_scratch,
-            received, image, far_const, index, far_hot, local, r, w, *state,
+            [vmem(wide, f32)] + near_scratch + far_scratch,
+            received, diag, own, slot, near_const, near_hot, far_const, index, far_hot, local, r, w, *state,
         )
         r, p, s, x, w, past = made[:6]
         if last:

time: 67.7 us -> 66.9 us (0.988)
  blocking collectives: 8.95 us -> 39.5 us
  waiting for transfers between devices: 26.9 us -> 7.52 us
  starting transfers between devices: 15 us -> 7.3 us
  Pallas kernels: 15.6 us -> 11.5 us
    all_to_all x1 -> x4, blocking collectives: 8.95 us -> 39.5 us  [exchange(): return lax.all_to_all(message, AXES, 0, 0)]
    all_to_all x4 -> x1, waiting for transfers between devices: 26.9 us -> 7.52 us  [exchange(): return lax.all_to_all(message, AXES, 0, 0)]
    all_to_all x4 -> x1, starting transfers between devices: 15 us -> 7.3 us  [exchange(): return lax.all_to_all(message, AXES, 0, 0)]
    pallas_call x10 -> x7, Pallas kernels: 15.6 us -> 11.5 us  [call(): pl.pallas_call(functools.partial(body, plan), out_shape=[(hbm if end else...]
  transfers between devices with their start and end apart: 4 -> 1, of which waited for: 4 -> 1; matrix products, arithmetic and copies ran while one was open for 0% -> 0% of each run, Pallas kernels for 12% -> 5%
where the time goes in v1:
time: 66.9 us; the launch traced here: 66.5 us
  blocking collectives  39.5 us (59%)
  Pallas kernels  11.5 us (17%)
  waiting for transfers between devices  7.52 us (11%)
  starting transfers between devices  7.3 us (11%)
    all_to_all x4, blocking collectives, exchange(): return lax.all_to_all(message, AXES, 0, 0)  39.5 us
    pallas_call x7, Pallas kernels, call(): pl.pallas_call(functools.partial(body, plan), out_shape=[(hbm if end else...  11.5 us
    all_to_all x1, waiting for transfers between devices, exchange(): return lax.all_to_all(message, AXES, 0, 0)  7.52 us
    all_to_all x1, starting transfers between devices, exchange(): return lax.all_to_all(message, AXES, 0, 0)  7.3 us
  transfers between devices with their start and end apart: 1, of which 1 were waited for; matrix products, arithmetic and copies ran while one was open for 0% of the time, Pallas kernels for 5%

profile of v1, /device:TPU:0, one launch (start us, length us, event | category | flops | bytes accessed | tf_op | source)
XLA Modules:
  0.0 66.5 jit_solution(15583275798417891845)
XLA Ops:
  0.6 1.8 %shard_map.96 = (f32[32,16,128]{2,1,0:T(8,128)}, f32[136,128]{1,0:T(8,128)S(1)}) custom-call(s32[24,128]{1,0:T(8,128)} %bitcast.12, s32[24,128]{1,0:T(8,128)} %bitcast.14, s32[24,128]{1,0:T(8,128)} %bitcast.16, f32[72,128]{1,0:T(8,128)} %bitcast.8, f32[1,1,1,2,3072]{4,3,2,1,0:T(2,128)} %radii_h.3, f32[48,128]{1,0:T(8,128)} %bitcast.10), custom_call_target="tpu_custom_call" | custom-call | tf_op jit(solution)/shard_map/pallas_call | solution.py:499
  2.4 7.3 %all-to-all-start = ((f32[32,16,128]{2,1,0:T(8,128)}), f32[32,16,128]{2,1,0:T(8,128)S(1)}, u32[]{:S(2)}, u32[]{:S(2)}) async-start(f32[32,16,128]{2,1,0:T(8,128)} %get-tuple-element.46), calls=%async_computation | async-start | bytes 524288 | tf_op jit(solution)/shard_map/all_to_all | solution.py:509
  9.7 3.1 %shard_map.95 = (f32[8,1024]{1,0:T(8,128)S(1)}, f32[9,24,128]{2,1,0:T(8,128)S(1)}, f32[8,1024]{1,0:T(8,128)S(1)}, f32[8,1024]{1,0:T(8,128)S(1)}, s32[24,128]{1,0...) custom-call(f32[4,4]{1,0:T(4,128)} %stiff_h.1, s32[24,128]{1,0:T(8,128)} %bitcast.13, ...), custom_call_target="tpu_custom_call" | custom-call | tf_op jit(solution)/shard_map/pallas_call | solution.py:499
  12.8 7.5 %all-to-all-done.received = f32[32,16,128]{2,1,0:T(8,128)S(1)} async-done(((f32[32,16,128]{2,1,0:T(8,128)}), f32[32,16,128]{2,1,0:T(8,128)S(1)}, u32[]{:S(2)}, u32[]{:S(2)}) %all-to-all-start) | async-done | bytes 262176 | tf_op jit(solution)/shard_map/all_to_all | solution.py:509
  20.3 1.2 %shard_map.97 = (f32[8,1024]{1,0:T(8,128)S(1)}, f32[32,8,128]{2,1,0:T(8,128)S(1)}, f32[9,24,128]{2,1,0:T(8,128)S(1)}, s32[24,128]{1,0:T(8,128)S(1)}, bf16[2176,2...) custom-call(f32[4,4]{1,0:T(4,128)S(1)} %get-tuple-element.45.stiff, f32[32,16,128]{2,1,0:T(8,128)S(1)} %all-to-all-done.received, ...), custom_call_target="tpu_custom_call" | custom-call | tf_op jit(solution)/shard_map/pallas_call | solution.py:499
  21.5 10.4 %all_to_all.25.refs_0_ = f32[32,8,128]{2,1,0:T(8,128)S(1)} all-to-all(f32[32,8,128]{2,1,0:T(8,128)S(1)} %get-tuple-element.50), channel_id=1, replica_groups=mesh['gx'=4,'gy'=2,'gz'=4] {'gx','gy','gz'}, dimensions={0} | all-to-all | bytes 262144 | tf_op jit(solution)/shard_map/all_to_all | solution.py:509
  31.9 1.6 %shard_map.98 = (f32[8,1024]{1,0:T(8,128)S(1)}, f32[8,1024]{1,0:T(8,128)S(1)}, f32[8,1024]{1,0:T(8,128)S(1)}, f32[8,1024]{1,0:T(8,128)S(1)}, f32[8,1024]{1,0:T(8...) custom-call(f32[32,8,128]{2,1,0:T(8,128)S(1)} %all_to_all.25.refs_0_, ...), custom_call_target="tpu_custom_call" | custom-call | tf_op jit(solution)/shard_map/pallas_call | solution.py:499
  33.5 10.0 %all_to_all.26.refs_0_ = f32[32,8,128]{2,1,0:T(8,128)S(1)} all-to-all(f32[32,8,128]{2,1,0:T(8,128)S(1)} %get-tuple-element.61), channel_id=1, replica_groups=mesh['gx'=4,'gy'=2,'gz'=4] {'gx','gy','gz'}, dimensions={0} | all-to-all | bytes 262144 | tf_op jit(solution)/shard_map/all_to_all | solution.py:509
  43.5 1.6 %shard_map.99 = (f32[8,1024]{1,0:T(8,128)S(1)}, f32[8,1024]{1,0:T(8,128)S(1)}, f32[8,1024]{1,0:T(8,128)S(1)}, f32[8,1024]{1,0:T(8,128)S(1)}, f32[8,1024]{1,0:T(8...) custom-call(f32[32,8,128]{2,1,0:T(8,128)S(1)} %all_to_all.26.refs_0_, ...), custom_call_target="tpu_custom_call" | custom-call | tf_op jit(solution)/shard_map/pallas_call | solution.py:499
  45.1 10.0 %all_to_all.27.refs_0_ = f32[32,8,128]{2,1,0:T(8,128)S(1)} all-to-all(f32[32,8,128]{2,1,0:T(8,128)S(1)} %get-tuple-element.70), channel_id=1, replica_groups=mesh['gx'=4,'gy'=2,'gz'=4] {'gx','gy','gz'}, dimensions={0} | all-to-all | bytes 262144 | tf_op jit(solution)/shard_map/all_to_all | solution.py:509
  55.1 1.5 %shard_map.100 = (f32[8,1024]{1,0:T(8,128)S(1)}, f32[8,1024]{1,0:T(8,128)S(1)}, f32[8,1024]{1,0:T(8,128)S(1)}, f32[8,1024]{1,0:T(8,128)S(1)}, f32[8,1024]{1,0:T(...) custom-call(f32[32,8,128]{2,1,0:T(8,128)S(1)} %all_to_all.27.refs_0_, ...), custom_call_target="tpu_custom_call" | custom-call | tf_op jit(solution)/shard_map/pallas_call | solution.py:499
  56.7 9.0 %all_to_all.28.received = f32[32,2,128]{2,1,0:T(2,128)S(1)} all-to-all(f32[32,2,128]{2,1,0:T(2,128)S(1)} %get-tuple-element.79), channel_id=1, replica_groups=mesh['gx'=4,'gy'=2,'gz'=4] {'gx','gy','gz'}, dimensions={0} | all-to-all | bytes 65536 | tf_op jit(solution)/shard_map/all_to_all | solution.py:509
  65.7 0.8 %shard_map.101 = (f32[48,128]{1,0:T(8,128)}, f32[48,128]{1,0:T(8,128)}) custom-call(f32[32,2,128]{2,1,0:T(2,128)S(1)} %all_to_all.28.received, f32[8,1024]{1,0:T(8,128)S(1)} %get-tuple-element.80.r, f32[8,1024]{1,0:T(8,128)S(1)} %get-tuple-element.81.w, f32[8,1024]{1,0:T(8,128)S(1)} %get-tuple-element.82.p, f32[8,1024]{1,0:T(8,128)S(1)} %get-tuple-element.83.s, ...), custom_call_target="tpu_custom_call" | custom-call | tf_op jit(solution)/shard_map/pallas_call | solution.py:499
Async XLA Ops:
  2.4 17.9 %all-to-all-start = ((f32[32,16,128]{2,1,0:T(8,128)}), f32[32,16,128]{2,1,0:T(8,128)S(1)}, u32[]{:S(2)}, u32[]{:S(2)}) async-start(f32[32,16,128]{2,1,0:T(8,128)} %get-tuple-element.46), calls=%async_computation | async-start | bytes 524288 | tf_op jit(solution)/shard_map/all_to_all | solution.py:509

commit v2 on v1

--- a/solution.py
+++ b/solution.py
@@ -26,7 +26,7 @@
         self.near = contacts - 26 * self.group
         self.near_tiles = -(-self.near // LANES)
         middle = self.near_tiles // 16 * 8
-        self.near_groups = [(0, middle), (middle, self.near_tiles)] if middle else [(0, self.near_tiles)]
+        self.near_groups = [(t, min(t + 8, self.near_tiles)) for t in range(0, self.near_tiles, 8)]
         self.tiles = contacts // LANES
         self.grain_tiles = grains // LANES
         self.rim_tiles = self.rim // LANES
@@ -57,12 +57,30 @@
 
 def lane_gather(tiles, index):
     low = jnp.bitwise_and(index, LANES - 1)
-    high = lax.shift_right_logical(index, 7)
-    total = jnp.zeros(tiles[0].shape, tiles[0].dtype)
-    for which, tile in enumerate(tiles):
-        found = jnp.take_along_axis(tile, low, axis=1, mode="promise_in_bounds")
-        total = jnp.where(high == which, found, total)
-    return total
+    found = [jnp.take_along_axis(t, low, axis=1, mode="promise_in_bounds") for t in tiles]
+    bit = LANES
+    while len(found) > 1:
+        odd = jnp.bitwise_and(index, bit) != 0
+        found = [jnp.where(odd, b, a) for a, b in zip(found[0::2], found[1::2])]
+        bit *= 2
+    return found[0]
+
+
+class Queue:
+    def __init__(self):
+        self.waiting = []
+
+    def add(self, left, hot, sums, start, stop):
+        step = 4 * LANES
+        for at in range(start, stop, step):
+            self.waiting.append((left, hot, sums, slice(at, min(at + step, stop))))
+
+    def run(self, count=None):
+        for _ in range(len(self.waiting) if count is None else min(count, len(self.waiting))):
+            left, hot, sums, lanes = self.waiting.pop(0)
+            sums.append(jnp.dot(left[:, lanes], hot[lanes, :], preferred_element_type=jnp.float32))
+            if len(sums) == 2:
+                sums[:] = [sums[0] + sums[1]]
 
 
 def spread(ref, row):
@@ -189,10 +207,11 @@
             message[where[e], 8 * t + FIELDS : 8 * t + 8, :] = packed[2 * t : 2 * t + 2, :]
 
 
-def near_part(plan, field, diag, own, slot, table, hot, image, seen, push, left):
+def near_part(plan, field, diag, own, slot, table, hot, image, seen, push, left, queue=None):
     tiles = [field[:, s * LANES : (s + 1) * LANES] for s in range(plan.grain_tiles)]
     parts = plan.grains // plan.rim
-    total = None
+    queue = queue or Queue()
+    found = []
     for start, stop in plan.near_groups:
         rows = stop - start
         base = 2 * start
@@ -200,6 +219,7 @@
             for t in range(rows):
                 at = (base + side * rows + t) * 8
                 seen[at : at + 8, :] = lane_gather(tiles, spread(index, start + t))
+                queue.run(1)
         one, two = base * 8, (base + rows) * 8
         first = [row_of(seen, one + c, 8, rows) for c in range(FIELDS)]
         second = [row_of(seen, two + c, 8, rows) for c in range(FIELDS)]
@@ -230,9 +250,9 @@
                     left[parts * 16 + q * 8 : parts * 16 + q * 8 + 16, lanes] = stacked(
                         lows[q], lows[q + 1]
                     )
-        lanes = slice(base * LANES, (base + 2 * rows) * LANES)
-        sums = jnp.dot(left[:, lanes], hot[lanes, :], preferred_element_type=jnp.float32)
-        total = sums if total is None else total + sums
+        queue.add(left, hot, found, base * LANES, (base + 2 * rows) * LANES)
+    queue.run()
+    (total,) = found
     for q in range(parts):
         lanes = slice(q * plan.rim, (q + 1) * plan.rim)
         at = parts * 16 + q * 8
@@ -286,7 +306,7 @@
     near_part(plan, field, diag, own, slot, table, hot, image, seen, push, left)
 
 
-def far_forces(plan, local, there, table, hot, push, left):
+def far_push(plan, local, there, table, hot, push, left, queue):
     rows = plan.far
     first = [row_of(local, c, 8, rows) for c in range(FIELDS)]
     second = [row_of(there, c, 8, rows) for c in range(FIELDS)]
@@ -303,7 +323,13 @@
         high, middle, low = three_parts(push[e * 8 : e * 8 + 8, :])
         left[0:16, lanes] = stacked(high, middle)
         left[16:32, lanes] = stacked(low, jnp.zeros_like(low))
-    total = jnp.dot(left[...], hot[...], preferred_element_type=jnp.float32)
+    found = []
+    queue.add(left, hot, found, 0, rows * LANES)
+    return found
+
+
+def far_total(found):
+    (total,) = found
     return total[0:8, :] + (total[8:16, :] + total[16:24, :])
 
 
@@ -391,7 +417,10 @@
         there[e * 8 : e * 8 + 8, :] = lane_gather(
             ghosts, jnp.broadcast_to(away[e : e + 1, :], (8, LANES))
         )
-    force = far_forces(plan, local, there, table, hot, push, left)
+    queue = Queue()
+    found = far_push(plan, local, there, table, hot, push, left, queue)
+    queue.run()
+    force = far_total(found)
     w[...] = image[...]
     w[:, 0 : plan.rim] = image[:, 0 : plan.rim] - force
     sums = partial_sums(field[...], w[...])
@@ -414,13 +443,17 @@
     else:
         (message,) = take(1)
     image, near_seen, near_push, near_left, there, push, left = take(7)
-    near_part(plan, w, diag, own, slot, near_const, near_hot, image, near_seen, near_push, near_left)
 
     where = plan.neighbours()
     for e in range(plan.far):
         there[e * 8 : e * 8 + 8, :] = received[where[e], :, :]
     sums = full_sums(received, FIELDS)
-    force = far_forces(plan, local, there, table, hot, push, left)
+    queue = Queue()
+    found = far_push(plan, local, there, table, hot, push, left, queue)
+    near_part(
+        plan, w, diag, own, slot, near_const, near_hot, image, near_seen, near_push, near_left, queue
+    )
+    force = far_total(found)
     q = jnp.concatenate(
         [image[:, 0 : plan.rim] - force, image[:, plan.rim :]], axis=1
     )

time: 66.9 us -> 65.8 us (0.984)
  Pallas kernels: 11.5 us -> 10 us
    pallas_call x7, Pallas kernels: 11.5 us -> 10 us  [call(): pl.pallas_call(functools.partial(body, plan), out_shape=[(hbm if end else...]
  transfers between devices with their start and end apart: 1 -> 1, of which waited for: 1 -> 1; matrix products, arithmetic and copies ran while one was open for 0% -> 0% of each run, Pallas kernels for 5% -> 4%
where the time goes in v2:
time: 65.8 us; the launch traced here: 65.3 us
  blocking collectives  39.5 us (60%)
  Pallas kernels  10 us (15%)
  waiting for transfers between devices  7.85 us (12%)
  starting transfers between devices  7.3 us (11%)
  between operations  0.66 us (1%)
    all_to_all x4, blocking collectives, exchange(): return lax.all_to_all(message, AXES, 0, 0)  39.5 us
    pallas_call x7, Pallas kernels, call(): pl.pallas_call(functools.partial(body, plan), out_shape=[(hbm if end else...  10 us
    all_to_all x1, waiting for transfers between devices, exchange(): return lax.all_to_all(message, AXES, 0, 0)  7.85 us
    all_to_all x1, starting transfers between devices, exchange(): return lax.all_to_all(message, AXES, 0, 0)  7.3 us
  transfers between devices with their start and end apart: 1, of which 1 were waited for; matrix products, arithmetic and copies ran while one was open for 0% of the time, Pallas kernels for 4%

profile of v2, /device:TPU:0, one launch (start us, length us, event | category | flops | bytes accessed | tf_op | source)
XLA Modules:
  0.0 65.3 jit_solution(7020333110099264331)
XLA Ops:
  0.6 1.8 %shard_map.96 = (f32[32,16,128]{2,1,0:T(8,128)}, f32[136,128]{1,0:T(8,128)S(1)}) custom-call(s32[24,128]{1,0:T(8,128)} %bitcast.12, s32[24,128]{1,0:T(8,128)} %bitcast.14, s32[24,128]{1,0:T(8,128)} %bitcast.16, f32[72,128]{1,0:T(8,128)} %bitcast.8, f32[1,1,1,2,3072]{4,3,2,1,0:T(2,128)} %radii_h.3, f32[48,128]{1,0:T(8,128)} %bitcast.10), custom_call_target="tpu_custom_call" | custom-call | tf_op jit(solution)/shard_map/pallas_call | solution.py:532
  2.4 7.3 %all-to-all-start = ((f32[32,16,128]{2,1,0:T(8,128)}), f32[32,16,128]{2,1,0:T(8,128)S(1)}, u32[]{:S(2)}, u32[]{:S(2)}) async-start(f32[32,16,128]{2,1,0:T(8,128)} %get-tuple-element.46), calls=%async_computation | async-start | bytes 524288 | tf_op jit(solution)/shard_map/all_to_all | solution.py:542
  9.7 2.7 %shard_map.95 = (f32[8,1024]{1,0:T(8,128)S(1)}, f32[9,24,128]{2,1,0:T(8,128)S(1)}, f32[8,1024]{1,0:T(8,128)S(1)}, f32[8,1024]{1,0:T(8,128)S(1)}, s32[24,128]{1,0...) custom-call(f32[4,4]{1,0:T(4,128)} %stiff_h.1, s32[24,128]{1,0:T(8,128)} %bitcast.13, ...), custom_call_target="tpu_custom_call" | custom-call | tf_op jit(solution)/shard_map/pallas_call | solution.py:532
  12.4 7.9 %all-to-all-done.received = f32[32,16,128]{2,1,0:T(8,128)S(1)} async-done(((f32[32,16,128]{2,1,0:T(8,128)}), f32[32,16,128]{2,1,0:T(8,128)S(1)}, u32[]{:S(2)}, u32[]{:S(2)}) %all-to-all-start) | async-done | bytes 262176 | tf_op jit(solution)/shard_map/all_to_all | solution.py:542
  20.3 1.2 %shard_map.97 = (f32[8,1024]{1,0:T(8,128)S(1)}, f32[32,8,128]{2,1,0:T(8,128)S(1)}, f32[9,24,128]{2,1,0:T(8,128)S(1)}, s32[24,128]{1,0:T(8,128)S(1)}, bf16[2176,2...) custom-call(f32[4,4]{1,0:T(4,128)S(1)} %get-tuple-element.45.stiff, f32[32,16,128]{2,1,0:T(8,128)S(1)} %all-to-all-done.received, ...), custom_call_target="tpu_custom_call" | custom-call | tf_op jit(solution)/shard_map/pallas_call | solution.py:532
  21.5 10.4 %all_to_all.25.refs_0_ = f32[32,8,128]{2,1,0:T(8,128)S(1)} all-to-all(f32[32,8,128]{2,1,0:T(8,128)S(1)} %get-tuple-element.50), channel_id=1, replica_groups=mesh['gx'=4,'gy'=2,'gz'=4] {'gx','gy','gz'}, dimensions={0} | all-to-all | bytes 262144 | tf_op jit(solution)/shard_map/all_to_all | solution.py:542
  31.9 1.2 %shard_map.98 = (f32[8,1024]{1,0:T(8,128)S(1)}, f32[8,1024]{1,0:T(8,128)S(1)}, f32[8,1024]{1,0:T(8,128)S(1)}, f32[8,1024]{1,0:T(8,128)S(1)}, f32[8,1024]{1,0:T(8...) custom-call(f32[32,8,128]{2,1,0:T(8,128)S(1)} %all_to_all.25.refs_0_, ...), custom_call_target="tpu_custom_call" | custom-call | tf_op jit(solution)/shard_map/pallas_call | solution.py:532
  33.1 10.0 %all_to_all.26.refs_0_ = f32[32,8,128]{2,1,0:T(8,128)S(1)} all-to-all(f32[32,8,128]{2,1,0:T(8,128)S(1)} %get-tuple-element.61), channel_id=1, replica_groups=mesh['gx'=4,'gy'=2,'gz'=4] {'gx','gy','gz'}, dimensions={0} | all-to-all | bytes 262144 | tf_op jit(solution)/shard_map/all_to_all | solution.py:542
  43.1 1.3 %shard_map.99 = (f32[8,1024]{1,0:T(8,128)S(1)}, f32[8,1024]{1,0:T(8,128)S(1)}, f32[8,1024]{1,0:T(8,128)S(1)}, f32[8,1024]{1,0:T(8,128)S(1)}, f32[8,1024]{1,0:T(8...) custom-call(f32[32,8,128]{2,1,0:T(8,128)S(1)} %all_to_all.26.refs_0_, ...), custom_call_target="tpu_custom_call" | custom-call | tf_op jit(solution)/shard_map/pallas_call | solution.py:532
  44.4 10.0 %all_to_all.27.refs_0_ = f32[32,8,128]{2,1,0:T(8,128)S(1)} all-to-all(f32[32,8,128]{2,1,0:T(8,128)S(1)} %get-tuple-element.70), channel_id=1, replica_groups=mesh['gx'=4,'gy'=2,'gz'=4] {'gx','gy','gz'}, dimensions={0} | all-to-all | bytes 262144 | tf_op jit(solution)/shard_map/all_to_all | solution.py:542
  54.4 1.1 %shard_map.100 = (f32[8,1024]{1,0:T(8,128)S(1)}, f32[8,1024]{1,0:T(8,128)S(1)}, f32[8,1024]{1,0:T(8,128)S(1)}, f32[8,1024]{1,0:T(8,128)S(1)}, f32[8,1024]{1,0:T(...) custom-call(f32[32,8,128]{2,1,0:T(8,128)S(1)} %all_to_all.27.refs_0_, ...), custom_call_target="tpu_custom_call" | custom-call | tf_op jit(solution)/shard_map/pallas_call | solution.py:532
  55.5 9.0 %all_to_all.28.received = f32[32,2,128]{2,1,0:T(2,128)S(1)} all-to-all(f32[32,2,128]{2,1,0:T(2,128)S(1)} %get-tuple-element.79), channel_id=1, replica_groups=mesh['gx'=4,'gy'=2,'gz'=4] {'gx','gy','gz'}, dimensions={0} | all-to-all | bytes 65536 | tf_op jit(solution)/shard_map/all_to_all | solution.py:542
  64.5 0.8 %shard_map.101 = (f32[48,128]{1,0:T(8,128)}, f32[48,128]{1,0:T(8,128)}) custom-call(f32[32,2,128]{2,1,0:T(2,128)S(1)} %all_to_all.28.received, f32[8,1024]{1,0:T(8,128)S(1)} %get-tuple-element.80.r, f32[8,1024]{1,0:T(8,128)S(1)} %get-tuple-element.81.w, f32[8,1024]{1,0:T(8,128)S(1)} %get-tuple-element.82.p, f32[8,1024]{1,0:T(8,128)S(1)} %get-tuple-element.83.s, ...), custom_call_target="tpu_custom_call" | custom-call | tf_op jit(solution)/shard_map/pallas_call | solution.py:532
Async XLA Ops:
  2.4 17.9 %all-to-all-start = ((f32[32,16,128]{2,1,0:T(8,128)}), f32[32,16,128]{2,1,0:T(8,128)S(1)}, u32[]{:S(2)}, u32[]{:S(2)}) async-start(f32[32,16,128]{2,1,0:T(8,128)} %get-tuple-element.46), calls=%async_computation | async-start | bytes 524288 | tf_op jit(solution)/shard_map/all_to_all | solution.py:542

commit v3 on v2

--- a/solution.py
+++ b/solution.py
@@ -40,7 +40,7 @@
         self.far = len(self.sides)
         most = max(len(groups) for groups in sides.values())
         self.half = -(-most * self.group // (LANES // 2)) * (LANES // 2)
-        assert self.half * 2 == LANES
+        assert self.half * 2 == LANES and self.rim_tiles == 2 and self.counts[2] % 2 == 0
 
     def neighbours(self):
         place = [lax.axis_index(axis) for axis in AXES]
@@ -168,9 +168,9 @@
             (own_h, own),
             (slot_h, slot),
             (kind_h, kind),
-            (normal_h, normal),
+            (normal_h, normal.at[pl.ds(0, 3 * plan.tiles), :]),
             (radii_h.at[0, 0, 0, :, lanes], radii),
-            (rhs_h, rhs),
+            (rhs_h, rhs.at[pl.ds(0, FIELDS * plan.grain_tiles), :]),
         ],
         sems,
     ):
@@ -202,9 +202,11 @@
             chunk = jnp.where(here, tile, chunk)
         mine[e * 8 : e * 8 + 8, :] = chunk
         packed = jnp.where(lane < plan.half, chunk, pltpu.roll(pltpu.roll(chunk, 4, 0), plan.half, 1))
-        for t in range(plan.rim_tiles):
-            message[where[e], 8 * t : 8 * t + FIELDS, :] = ghosts[t]
-            message[where[e], 8 * t + FIELDS : 8 * t + 8, :] = packed[2 * t : 2 * t + 2, :]
+        for i in range(2):
+            message[where[e], i, :, :] = packed[2 * i : 2 * i + 2, :]
+    for d in range(plan.devices):
+        for i in range(FIELDS // 2):
+            message[d, 2 + i, :, :] = ghosts[d % 2][2 * i : 2 * i + 2, :]
 
 
 def near_part(plan, field, diag, own, slot, table, hot, image, seen, push, left, queue=None):
@@ -266,6 +268,7 @@
     image, table, field, diag, own, slot, stiff, hot, kind, radii, rhs, ground, seen, push, left, sems,
 ):
     rows = plan.near_tiles
+    lines = pl.ds(0, FIELDS * plan.grain_tiles)
     copies = fetch(
         [
             (stiff_h, stiff),
@@ -273,8 +276,8 @@
             (slot_h, slot),
             (kind_h, kind),
             (radii_h.at[0, 0, 0], radii),
-            (rhs_h, rhs),
-            (diag_h, ground),
+            (rhs_h, rhs.at[lines, :]),
+            (diag_h, ground.at[lines, :]),
         ]
         + [(normal_h.at[pl.ds(c * plan.tiles, plan.tiles), :], table.at[c]) for c in range(3)],
         sems,
@@ -379,22 +382,15 @@
     return gamma / (delta + beta * (mixed + beta * energy)), beta
 
 
-def far_first(
-    plan, stiff, received, mine, field, image,
-    w, message, table, index, hot, local, merged, there, push, left,
+def far_tables(
+    plan, stiff, received, mine, field, table, index, away, hot, local, merged,
 ):
     lane8 = lax.broadcasted_iota(jnp.int32, (8, LANES), 1)
     where = plan.neighbours()
     rows = plan.far
     for e in range(rows):
         own = pltpu.roll(mine[e * 8 : e * 8 + 8, :], plan.half, 1)
-        packed = jnp.concatenate(
-            [
-                received[where[e], 8 * t + FIELDS : 8 * t + 8, :]
-                for t in range(plan.rim_tiles)
-            ],
-            axis=0,
-        )
+        packed = jnp.concatenate([received[where[e], 0], received[where[e], 1]], axis=0)
         chunk = jnp.concatenate([packed, pltpu.roll(packed, plan.half, 1)], axis=0)
         merged[e * 8 : e * 8 + 8, :] = jnp.where(lane8 < plan.half, chunk, own)
     mirror = lax.broadcasted_iota(jnp.int32, (rows, LANES), 1) < plan.half
@@ -406,16 +402,31 @@
     for k, value in enumerate(coefficients(stiff, row[2], plan.types)):
         table[5 + k, 0:rows, :] = value
     here = jnp.where(mirror, row[1], row[0])
-    away = jnp.where(mirror, row[0], row[1]).astype(jnp.int32)
     index[0:rows, :] = here.astype(jnp.int32)
+    away[0:rows, :] = jnp.where(mirror, row[0], row[1]).astype(jnp.int32)
     make = one_hot(here, plan.rim)
     tiles = [field[:, t * LANES : (t + 1) * LANES] for t in range(plan.rim_tiles)]
     for e in range(rows):
         hot[e * LANES : (e + 1) * LANES, :] = make(e)
         local[e * 8 : e * 8 + 8, :] = lane_gather(tiles, spread(index, e))
-        ghosts = [received[where[e], 8 * t : 8 * t + 8, :] for t in range(plan.rim_tiles)]
-        there[e * 8 : e * 8 + 8, :] = lane_gather(
-            ghosts, jnp.broadcast_to(away[e : e + 1, :], (8, LANES))
+
+
+def far_first(
+    plan, received, swapped, table, index, away, hot, local, field, image,
+    w, message, local_new, there, push, left,
+):
+    where = plan.neighbours()
+    half = lax.rem(lax.axis_index(AXES[2]), 2)
+    for e in range(plan.far):
+        wanted = spread(away, e)
+        low = jnp.bitwise_and(wanted, LANES - 1)
+        found = []
+        for source in (received, swapped):
+            rows = [source[where[e], 2 + i] for i in (0, 1, 2, 2)]
+            tile = jnp.concatenate(rows, axis=0)
+            found.append(jnp.take_along_axis(tile, low, axis=1, mode="promise_in_bounds"))
+        there[e * 8 : e * 8 + 8, :] = jnp.where(
+            lax.shift_right_logical(wanted, 7) == half, found[0], found[1]
         )
     queue = Queue()
     found = far_push(plan, local, there, table, hot, push, left, queue)
@@ -424,7 +435,7 @@
     w[...] = image[...]
     w[:, 0 : plan.rim] = image[:, 0 : plan.rim] - force
     sums = partial_sums(field[...], w[...])
-    send_rim(plan, w, index, sums, message, local)
+    send_rim(plan, w, index, sums, message, local_new)
 
 
 def far_step(plan, number, *refs):
@@ -492,7 +503,8 @@
         there = pl.ds(t, FIELDS, stride=plan.grain_tiles), slice(None)
         x_last[there] = x[here] + alpha * (r[here] + beta * p[here])
         r_last[there] = r[here] - alpha * (w[here] + beta * s[here])
-    for copy in fetch([(x_last, x_out), (r_last, r_out)], sems):
+    lines = pl.ds(0, FIELDS * plan.grain_tiles)
+    for copy in fetch([(x_last.at[lines, :], x_out), (r_last.at[lines, :], r_out)], sems):
         copy.wait()
 
 
@@ -513,12 +525,13 @@
     kind = contact_type.reshape(plan.tiles, LANES)
     normal = contact_normal.reshape(3 * plan.tiles, LANES)
     lines = (FIELDS * plan.grain_tiles, LANES)
+    more_lines = (8 * plan.grain_tiles, LANES)
     rhs = right_side.reshape(lines)
     ground = grain_diag.reshape(lines)
     f32, bf16, i32 = jnp.float32, jnp.bfloat16, jnp.int32
     vmem, hbm, dma = pltpu.MemorySpace.VMEM, pltpu.MemorySpace.HBM, pltpu.SemaphoreType.DMA
     wide = (8, plan.grains)
-    far = (plan.far * 8, LANES)
+    far = (-(-plan.far // 8) * 64, LANES)
     far_table = (9, -(-plan.far // 8) * 8, LANES)
     near_table = (9, plan.tiles, LANES)
     table = (plan.tiles, LANES)
@@ -543,22 +556,22 @@
 
     tile = (plan.devices, 8, LANES)
     near_scratch = [
-        vmem((near_rows * 8, LANES), f32),
-        vmem((near_rows * 8, LANES), f32),
+        vmem((near_rows * 8 + 64, LANES), f32),
+        vmem((near_rows * 8 + 64, LANES), f32),
         vmem((parts * 24, near_rows * LANES), bf16),
     ]
     far_scratch = [vmem(far, f32), vmem(far, f32), vmem((32, plan.far * LANES), bf16)]
 
     message, mine = call(
         send_setup,
-        [((plan.devices, 8 * plan.rim_tiles, LANES), f32), (far, f32)],
+        [((plan.devices, 2 + FIELDS // 2, 2, LANES), f32), (far, f32)],
         [
             vmem(table, i32),
             vmem(table, i32),
             vmem(table, i32),
-            vmem(normal.shape, f32),
+            vmem((8 * plan.tiles, LANES), f32),
             vmem((2, rest), f32),
-            vmem(lines, f32),
+            vmem(more_lines, f32),
             vmem((rest // LANES * 8, LANES), f32),
             dma((6,)),
         ],
@@ -578,24 +591,32 @@
             (stiffness.shape, f32),
             ((near_rows * LANES, plan.rim), bf16),
         ],
-        [vmem(table, i32), vmem((2, plan.contacts), f32), vmem(lines, f32), vmem(lines, f32)]
+        [vmem(table, i32), vmem((2, plan.contacts), f32), vmem(more_lines, f32), vmem(more_lines, f32)]
         + near_scratch
         + [dma((10,))],
         stiffness, own, slot, kind, normal, contact_radii, rhs, ground,
         raw=True,
     )
-    w, message, far_const, index, far_hot, local = call(
-        far_first,
+    pairs = [(i, i ^ 1) for i in range(plan.counts[2])]
+    received, image = lax.optimization_barrier((received, image))
+    swapped = lax.ppermute(received, AXES[2], pairs)
+    far_const, index, away, far_hot, local = call(
+        far_tables,
         [
-            (wide, f32),
-            (tile, f32),
             (far_table, f32),
+            (far_table[1:], i32),
             (far_table[1:], i32),
             ((plan.far * LANES, plan.rim), bf16),
             (far, f32),
         ],
-        [vmem(far, f32)] + far_scratch,
-        stiff, received, mine, field, image,
+        [vmem(far, f32)],
+        stiff, received, mine, field,
+    )
+    w, message, local = call(
+        far_first,
+        [(wide, f32), (tile, f32), (far, f32)],
+        far_scratch,
+        received, swapped, far_const, index, away, far_hot, local, field, image,
     )
     r = field
     state = ()
@@ -623,7 +644,7 @@
     solution_field, residual = call(
         finish,
         [(lines, f32)] * 2,
-        [vmem(lines, f32), vmem(lines, f32), dma((2,))],
+        [vmem(more_lines, f32), vmem(more_lines, f32), dma((2,))],
         received, r, w, p, s, x, past,
         end=True,
     )

time: 65.8 us -> 64.6 us (0.982)
  waiting for transfers between devices: 7.85 us -> 6.13 us
    all_to_all x1, waiting for transfers between devices: 7.85 us -> 5.83 us  [exchange(): return lax.all_to_all(message, AXES, 0, 0)]
    pallas_call x7 -> x8, Pallas kernels: 10 us -> 10.2 us  [call(): pl.pallas_call(functools.partial(body, plan), out_shape=[(hbm if end else...]
  transfers between devices with their start and end apart: 1 -> 2, of which waited for: 1 -> 2; matrix products, arithmetic and copies ran while one was open for 0% -> 0% of each run, Pallas kernels for 4% -> 5%
where the time goes in v3:
time: 64.6 us; the launch traced here: 64.1 us
  blocking collectives  39.4 us (61%)
  Pallas kernels  10.2 us (16%)
  starting transfers between devices  7.69 us (12%)
  waiting for transfers between devices  6.13 us (9%)
  between operations  0.67 us (1%)
    all_to_all x4, blocking collectives, exchange(): return lax.all_to_all(message, AXES, 0, 0)  39.4 us
    pallas_call x8, Pallas kernels, call(): pl.pallas_call(functools.partial(body, plan), out_shape=[(hbm if end else...  10.2 us
    all_to_all x1, starting transfers between devices, exchange(): return lax.all_to_all(message, AXES, 0, 0)  7.3 us
    all_to_all x1, waiting for transfers between devices, exchange(): return lax.all_to_all(message, AXES, 0, 0)  5.83 us
  transfers between devices with their start and end apart: 2, of which 2 were waited for; matrix products, arithmetic and copies ran while one was open for 0% of the time, Pallas kernels for 5%

profile of v3, /device:TPU:0, one launch (start us, length us, event | category | flops | bytes accessed | tf_op | source)
XLA Modules:
  0.0 64.1 jit_solution(16487449623776441578)
XLA Ops:
  0.6 1.7 %shard_map.95 = (f32[32,5,2,128]{3,2,1,0:T(2,128)}, f32[192,128]{1,0:T(8,128)S(1)}) custom-call(s32[24,128]{1,0:T(8,128)} %bitcast.12, s32[24,128]{1,0:T(8,128)} %bitcast.14, s32[24,128]{1,0:T(8,128)} %bitcast.16, f32[72,128]{1,0:T(8,128)} %bitcast.8, f32[1,1,1,2,3072]{4,3,2,1,0:T(2,128)} %radii_h.3, f32[48,128]{1,0:T(8,128)} %bitcast.10), custom_call_target="tpu_custom_call" | custom-call | tf_op jit(solution)/shard_map/pallas_call | solution.py:545
  2.4 7.3 %all-to-all-start = ((f32[32,5,2,128]{3,2,1,0:T(2,128)}), f32[32,5,2,128]{3,2,1,0:T(2,128)S(1)}, u32[]{:S(2)}, u32[]{:S(2)}) async-start(f32[32,5,2,128]{3,2,1,0:T(2,128)} %get-tuple-element.49), calls=%async_computation | async-start | bytes 327680 | tf_op jit(solution)/shard_map/all_to_all | solution.py:555
  9.7 2.7 %shard_map.96 = (f32[8,1024]{1,0:T(8,128)S(1)}, f32[9,24,128]{2,1,0:T(8,128)S(1)}, f32[8,1024]{1,0:T(8,128)S(1)}, f32[8,1024]{1,0:T(8,128)S(1)}, s32[24,128]{1,0...) custom-call(f32[4,4]{1,0:T(4,128)} %stiff_h.1, s32[24,128]{1,0:T(8,128)} %bitcast.13, ...), custom_call_target="tpu_custom_call" | custom-call | tf_op jit(solution)/shard_map/pallas_call | solution.py:545
  12.4 5.8 %all-to-all-done.received = f32[32,5,2,128]{3,2,1,0:T(2,128)S(1)} async-done(((f32[32,5,2,128]{3,2,1,0:T(2,128)}), f32[32,5,2,128]{3,2,1,0:T(2,128)S(1)}, u32[]{:S(2)}, u32[]{:S(2)}) %all-to-all-start) | async-done | bytes 163872 | tf_op jit(solution)/shard_map/all_to_all | solution.py:555
  18.2 0.4 collective-permute-start
  18.6 0.7 %shard_map.97 = (f32[9,24,128]{2,1,0:T(8,128)S(1)}, s32[24,128]{1,0:T(8,128)S(1)}, s32[24,128]{1,0:T(8,128)S(1)}, bf16[2176,256]{1,0:T(8,128)(2,1)S(1)}, f32[192,128]{1,0:T(8,128)S(1)}) custom-call(f32[4,4]{1,0:T(4,128)S(1)} %get-tuple-element.52.stiff, f32[32,5,2,128]{3,2,1,0:T(2,128)S(1)} %all-to-all-done.received, f32[192,128]{1,0:T(8,128)S(1)} %get-tuple-element.53.mine, ...), custom_call_target="tpu_custom_call" | custom-call | tf_op jit(solution)/shard_map/pallas_call | solution.py:545
  19.3 0.3 collective-permute-done.swapped
  19.7 0.7 %shard_map.98 = (f32[8,1024]{1,0:T(8,128)S(1)}, f32[32,8,128]{2,1,0:T(8,128)S(1)}, f32[192,128]{1,0:T(8,128)S(1)}) custom-call(f32[32,5,2,128]{3,2,1,0:T(2,128)S(1)} %all-to-all-done.received, f32[32,5,2,128]{3,2,1,0:T(2,128)S(1)} %collective-permute-done.swapped, f32[9,24,128]{2,1,0:T(8,128)S(1)} %get-tuple-element.55.table.refs_6_, ...), custom_call_target="tpu_custom_call" | custom-call | tf_op jit(solution)/shard_map/pallas_call | solution.py:545
  20.3 10.3 %all_to_all.25.refs_0_ = f32[32,8,128]{2,1,0:T(8,128)S(1)} all-to-all(f32[32,8,128]{2,1,0:T(8,128)S(1)} %get-tuple-element.61), channel_id=1, replica_groups=mesh['gx'=4,'gy'=2,'gz'=4] {'gx','gy','gz'}, dimensions={0} | all-to-all | bytes 262144 | tf_op jit(solution)/shard_map/all_to_all | solution.py:555
  30.7 1.2 %shard_map.99 = (f32[8,1024]{1,0:T(8,128)S(1)}, f32[8,1024]{1,0:T(8,128)S(1)}, f32[8,1024]{1,0:T(8,128)S(1)}, f32[8,1024]{1,0:T(8,128)S(1)}, f32[8,1024]{1,0:T(8...) custom-call(f32[32,8,128]{2,1,0:T(8,128)S(1)} %all_to_all.25.refs_0_, ...), custom_call_target="tpu_custom_call" | custom-call | tf_op jit(solution)/shard_map/pallas_call | solution.py:545
  31.9 10.0 %all_to_all.26.refs_0_ = f32[32,8,128]{2,1,0:T(8,128)S(1)} all-to-all(f32[32,8,128]{2,1,0:T(8,128)S(1)} %get-tuple-element.69), channel_id=1, replica_groups=mesh['gx'=4,'gy'=2,'gz'=4] {'gx','gy','gz'}, dimensions={0} | all-to-all | bytes 262144 | tf_op jit(solution)/shard_map/all_to_all | solution.py:555
  41.9 1.3 %shard_map.100 = (f32[8,1024]{1,0:T(8,128)S(1)}, f32[8,1024]{1,0:T(8,128)S(1)}, f32[8,1024]{1,0:T(8,128)S(1)}, f32[8,1024]{1,0:T(8,128)S(1)}, f32[8,1024]{1,0:T(...) custom-call(f32[32,8,128]{2,1,0:T(8,128)S(1)} %all_to_all.26.refs_0_, ...), custom_call_target="tpu_custom_call" | custom-call | tf_op jit(solution)/shard_map/pallas_call | solution.py:545
  43.2 10.0 %all_to_all.27.refs_0_ = f32[32,8,128]{2,1,0:T(8,128)S(1)} all-to-all(f32[32,8,128]{2,1,0:T(8,128)S(1)} %get-tuple-element.78), channel_id=1, replica_groups=mesh['gx'=4,'gy'=2,'gz'=4] {'gx','gy','gz'}, dimensions={0} | all-to-all | bytes 262144 | tf_op jit(solution)/shard_map/all_to_all | solution.py:555
  53.2 1.1 %shard_map.101 = (f32[8,1024]{1,0:T(8,128)S(1)}, f32[8,1024]{1,0:T(8,128)S(1)}, f32[8,1024]{1,0:T(8,128)S(1)}, f32[8,1024]{1,0:T(8,128)S(1)}, f32[8,1024]{1,0:T(...) custom-call(f32[32,8,128]{2,1,0:T(8,128)S(1)} %all_to_all.27.refs_0_, ...), custom_call_target="tpu_custom_call" | custom-call | tf_op jit(solution)/shard_map/pallas_call | solution.py:545
  54.3 9.0 %all_to_all.28.received = f32[32,2,128]{2,1,0:T(2,128)S(1)} all-to-all(f32[32,2,128]{2,1,0:T(2,128)S(1)} %get-tuple-element.87), channel_id=1, replica_groups=mesh['gx'=4,'gy'=2,'gz'=4] {'gx','gy','gz'}, dimensions={0} | all-to-all | bytes 65536 | tf_op jit(solution)/shard_map/all_to_all | solution.py:555
  63.3 0.8 %shard_map.102 = (f32[48,128]{1,0:T(8,128)}, f32[48,128]{1,0:T(8,128)}) custom-call(f32[32,2,128]{2,1,0:T(2,128)S(1)} %all_to_all.28.received, f32[8,1024]{1,0:T(8,128)S(1)} %get-tuple-element.88.r, f32[8,1024]{1,0:T(8,128)S(1)} %get-tuple-element.89.w, f32[8,1024]{1,0:T(8,128)S(1)} %get-tuple-element.90.p, f32[8,1024]{1,0:T(8,128)S(1)} %get-tuple-element.91.s, ...), custom_call_target="tpu_custom_call" | custom-call | tf_op jit(solution)/shard_map/pallas_call | solution.py:545
Async XLA Ops:
  2.4 15.9 %all-to-all-start = ((f32[32,5,2,128]{3,2,1,0:T(2,128)}), f32[32,5,2,128]{3,2,1,0:T(2,128)S(1)}, u32[]{:S(2)}, u32[]{:S(2)}) async-start(f32[32,5,2,128]{3,2,1,0:T(2,128)} %get-tuple-element.49), calls=%async_computation | async-start | bytes 327680 | tf_op jit(solution)/shard_map/all_to_all | solution.py:555
  18.2 1.4 %collective-permute-start = (f32[32,5,2,128]{3,2,1,0:T(2,128)S(1)}, f32[32,5,2,128]{3,2,1,0:T(2,128)S(1)}, u32[]{:S(2)}, u32[]{:S(2)}) collective-permute-start(f32[32,5,2,128]{3,2,1,0:T(2,128)S(1)} %all-to-all-done.received), channel_id=1, source_target_pairs={{0,1},{1,0},{2,3},{3,2},{4,5},{5,4},{6,7},{7,6},{8,9},{9,8},{10,11... | collective-permute-start | bytes 491528 | tf_op jit(solution)/shard_map/ppermute | solution.py:602

commit v4 on v3

--- a/solution.py
+++ b/solution.py
@@ -71,7 +71,7 @@
         self.waiting = []
 
     def add(self, left, hot, sums, start, stop):
-        step = 4 * LANES
+        step = 8 * LANES
         for at in range(start, stop, step):
             self.waiting.append((left, hot, sums, slice(at, min(at + step, stop))))
 
@@ -209,7 +209,7 @@
             message[d, 2 + i, :, :] = ghosts[d % 2][2 * i : 2 * i + 2, :]
 
 
-def near_part(plan, field, diag, own, slot, table, hot, image, seen, push, left, queue=None):
+def near_part(plan, field, diag, own, slot, table, hot, image, seen, push, left, queue=None, then=None):
     tiles = [field[:, s * LANES : (s + 1) * LANES] for s in range(plan.grain_tiles)]
     parts = plan.grains // plan.rim
     queue = queue or Queue()
@@ -222,6 +222,8 @@
                 at = (base + side * rows + t) * 8
                 seen[at : at + 8, :] = lane_gather(tiles, spread(index, start + t))
                 queue.run(1)
+        if then and start == 0:
+            then()
         one, two = base * 8, (base + rows) * 8
         first = [row_of(seen, one + c, 8, rows) for c in range(FIELDS)]
         second = [row_of(seen, two + c, 8, rows) for c in range(FIELDS)]
@@ -243,11 +245,11 @@
                 split = three_parts(push[at * 8 : at * 8 + 8, :])
                 part = lax.shift_right_logical(spread(index, start + t), plan.rim_bits)
                 lows = []
+                pair = stacked(split[0], split[1])
                 for q in range(parts):
-                    here = part == q
-                    high, middle, low = [jnp.where(here, x, 0.0) for x in split]
-                    left[q * 16 : q * 16 + 16, lanes] = stacked(high, middle)
-                    lows.append(low)
+                    here = jnp.where(part == q, 1.0, 0.0)
+                    left[q * 16 : q * 16 + 16, lanes] = pair * stacked(here, here)
+                    lows.append(split[2] * here)
                 for q in range(0, parts, 2):
                     left[parts * 16 + q * 8 : parts * 16 + q * 8 + 16, lanes] = stacked(
                         lows[q], lows[q + 1]
@@ -374,6 +376,24 @@
         for half in (jnp.where(low, total, 0.0), jnp.where(low, 0.0, total)):
             found.append(jnp.sum(half, axis=1, keepdims=True))
     return found[0], found[2], found[1], found[3]
+
+
+def one_row(sums):
+    upper, lower = sums
+    quarter = LANES // 4
+    lane = lax.broadcasted_iota(jnp.int32, (8, LANES), 1)
+    upper, lower = [jnp.broadcast_to(x, (8, LANES)) for x in (upper, lower)]
+    upper = upper + pltpu.roll(upper, quarter, 1)
+    lower = lower + pltpu.roll(lower, LANES - quarter, 1)
+    return jnp.where(jnp.bitwise_and(lane, quarter) != 0, upper, lower)[0:1, :]
+
+
+def row_sums(received):
+    total = jnp.sum(received[:, 0, :], axis=0, keepdims=True)
+    part = lax.broadcasted_iota(jnp.int32, (1, LANES), 1) // (LANES // 4)
+    return [
+        jnp.sum(jnp.where(part == q, total, 0.0), axis=1, keepdims=True) for q in (1, 0, 3, 2)
+    ]
 
 
 def step_sizes(sums, past):
@@ -460,10 +480,12 @@
         there[e * 8 : e * 8 + 8, :] = received[where[e], :, :]
     sums = full_sums(received, FIELDS)
     queue = Queue()
-    found = far_push(plan, local, there, table, hot, push, left, queue)
+    kept = []
     near_part(
-        plan, w, diag, own, slot, near_const, near_hot, image, near_seen, near_push, near_left, queue
-    )
+        plan, w, diag, own, slot, near_const, near_hot, image, near_seen, near_push, near_left, queue,
+        lambda: kept.append(far_push(plan, local, there, table, hot, push, left, queue)),
+    )
+    (found,) = kept
     force = far_total(found)
     q = jnp.concatenate(
         [image[:, 0 : plan.rim] - force, image[:, plan.rim :]], axis=1
@@ -492,12 +514,11 @@
         z_new[...] = z_now
         send_rim(plan, w_new, index, sums, message, local_new)
     else:
-        base = jnp.concatenate(sums, axis=0)
-        message[...] = jnp.broadcast_to(base[None], message.shape)
+        message[...] = jnp.broadcast_to(one_row(sums)[None], message.shape)
 
 
 def finish(plan, received, r, w, p, s, x, past, x_out, r_out, x_last, r_last, sems):
-    alpha, beta = step_sizes(full_sums(received, 0), past)
+    alpha, beta = step_sizes(row_sums(received), past)
     for t in range(plan.grain_tiles):
         here = slice(0, FIELDS), slice(t * LANES, (t + 1) * LANES)
         there = pl.ds(t, FIELDS, stride=plan.grain_tiles), slice(None)
@@ -625,7 +646,7 @@
         last = number == ITERS - 2
         outs = [(wide, f32)] * 5 + [((8, LANES), f32)]
         if last:
-            outs = outs + [((plan.devices, 2, LANES), f32)]
+            outs = outs + [((plan.devices, 1, LANES), f32)]
         else:
             outs = outs + [(wide, f32), (tile, f32), (far, f32)]
         made = call(

time: 64.6 us -> 64.5 us (level)
  no operation moved by 1% of the time
where the time goes in v4:
time: 64.5 us; the launch traced here: 64.1 us
  blocking collectives  39.3 us (61%)
  Pallas kernels  10.3 us (16%)
  starting transfers between devices  7.69 us (12%)
  waiting for transfers between devices  6.14 us (10%)
  between operations  0.67 us (1%)
    all_to_all x4, blocking collectives, exchange(): return lax.all_to_all(message, AXES, 0, 0)  39.3 us
    pallas_call x8, Pallas kernels, call(): pl.pallas_call(functools.partial(body, plan), out_shape=[(hbm if end else...  10.3 us
    all_to_all x1, starting transfers between devices, exchange(): return lax.all_to_all(message, AXES, 0, 0)  7.3 us
    all_to_all x1, waiting for transfers between devices, exchange(): return lax.all_to_all(message, AXES, 0, 0)  5.83 us
  transfers between devices with their start and end apart: 2, of which 2 were waited for; matrix products, arithmetic and copies ran while one was open for 0% of the time, Pallas kernels for 5%

profile of v4, /device:TPU:0, one launch (start us, length us, event | category | flops | bytes accessed | tf_op | source)
XLA Modules:
  0.0 64.1 jit_solution(5224263023153098057)
XLA Ops:
  0.6 1.7 %shard_map.95 = (f32[32,5,2,128]{3,2,1,0:T(2,128)}, f32[192,128]{1,0:T(8,128)S(1)}) custom-call(s32[24,128]{1,0:T(8,128)} %bitcast.12, s32[24,128]{1,0:T(8,128)} %bitcast.14, s32[24,128]{1,0:T(8,128)} %bitcast.16, f32[72,128]{1,0:T(8,128)} %bitcast.8, f32[1,1,1,2,3072]{4,3,2,1,0:T(2,128)} %radii_h.3, f32[48,128]{1,0:T(8,128)} %bitcast.10), custom_call_target="tpu_custom_call" | custom-call | tf_op jit(solution)/shard_map/pallas_call | solution.py:566
  2.4 7.3 %all-to-all-start = ((f32[32,5,2,128]{3,2,1,0:T(2,128)}), f32[32,5,2,128]{3,2,1,0:T(2,128)S(1)}, u32[]{:S(2)}, u32[]{:S(2)}) async-start(f32[32,5,2,128]{3,2,1,0:T(2,128)} %get-tuple-element.49), calls=%async_computation | async-start | bytes 327680 | tf_op jit(solution)/shard_map/all_to_all | solution.py:576
  9.7 2.7 %shard_map.96 = (f32[8,1024]{1,0:T(8,128)S(1)}, f32[9,24,128]{2,1,0:T(8,128)S(1)}, f32[8,1024]{1,0:T(8,128)S(1)}, f32[8,1024]{1,0:T(8,128)S(1)}, s32[24,128]{1,0...) custom-call(f32[4,4]{1,0:T(4,128)} %stiff_h.1, s32[24,128]{1,0:T(8,128)} %bitcast.13, ...), custom_call_target="tpu_custom_call" | custom-call | tf_op jit(solution)/shard_map/pallas_call | solution.py:566
  12.4 5.8 %all-to-all-done.received = f32[32,5,2,128]{3,2,1,0:T(2,128)S(1)} async-done(((f32[32,5,2,128]{3,2,1,0:T(2,128)}), f32[32,5,2,128]{3,2,1,0:T(2,128)S(1)}, u32[]{:S(2)}, u32[]{:S(2)}) %all-to-all-start) | async-done | bytes 163872 | tf_op jit(solution)/shard_map/all_to_all | solution.py:576
  18.2 0.4 collective-permute-start
  18.6 0.7 %shard_map.97 = (f32[9,24,128]{2,1,0:T(8,128)S(1)}, s32[24,128]{1,0:T(8,128)S(1)}, s32[24,128]{1,0:T(8,128)S(1)}, bf16[2176,256]{1,0:T(8,128)(2,1)S(1)}, f32[192,128]{1,0:T(8,128)S(1)}) custom-call(f32[4,4]{1,0:T(4,128)S(1)} %get-tuple-element.52.stiff, f32[32,5,2,128]{3,2,1,0:T(2,128)S(1)} %all-to-all-done.received, f32[192,128]{1,0:T(8,128)S(1)} %get-tuple-element.53.mine, ...), custom_call_target="tpu_custom_call" | custom-call | tf_op jit(solution)/shard_map/pallas_call | solution.py:566
  19.3 0.3 collective-permute-done.swapped
  19.7 0.7 %shard_map.98 = (f32[8,1024]{1,0:T(8,128)S(1)}, f32[32,8,128]{2,1,0:T(8,128)S(1)}, f32[192,128]{1,0:T(8,128)S(1)}) custom-call(f32[32,5,2,128]{3,2,1,0:T(2,128)S(1)} %all-to-all-done.received, f32[32,5,2,128]{3,2,1,0:T(2,128)S(1)} %collective-permute-done.swapped, f32[9,24,128]{2,1,0:T(8,128)S(1)} %get-tuple-element.55.table.refs_6_, ...), custom_call_target="tpu_custom_call" | custom-call | tf_op jit(solution)/shard_map/pallas_call | solution.py:566
  20.3 10.3 %all_to_all.25.refs_0_ = f32[32,8,128]{2,1,0:T(8,128)S(1)} all-to-all(f32[32,8,128]{2,1,0:T(8,128)S(1)} %get-tuple-element.61), channel_id=1, replica_groups=mesh['gx'=4,'gy'=2,'gz'=4] {'gx','gy','gz'}, dimensions={0} | all-to-all | bytes 262144 | tf_op jit(solution)/shard_map/all_to_all | solution.py:576
  30.7 1.2 %shard_map.99 = (f32[8,1024]{1,0:T(8,128)S(1)}, f32[8,1024]{1,0:T(8,128)S(1)}, f32[8,1024]{1,0:T(8,128)S(1)}, f32[8,1024]{1,0:T(8,128)S(1)}, f32[8,1024]{1,0:T(8...) custom-call(f32[32,8,128]{2,1,0:T(8,128)S(1)} %all_to_all.25.refs_0_, ...), custom_call_target="tpu_custom_call" | custom-call | tf_op jit(solution)/shard_map/pallas_call | solution.py:566
  31.9 10.0 %all_to_all.26.refs_0_ = f32[32,8,128]{2,1,0:T(8,128)S(1)} all-to-all(f32[32,8,128]{2,1,0:T(8,128)S(1)} %get-tuple-element.69), channel_id=1, replica_groups=mesh['gx'=4,'gy'=2,'gz'=4] {'gx','gy','gz'}, dimensions={0} | all-to-all | bytes 262144 | tf_op jit(solution)/shard_map/all_to_all | solution.py:576
  41.9 1.3 %shard_map.100 = (f32[8,1024]{1,0:T(8,128)S(1)}, f32[8,1024]{1,0:T(8,128)S(1)}, f32[8,1024]{1,0:T(8,128)S(1)}, f32[8,1024]{1,0:T(8,128)S(1)}, f32[8,1024]{1,0:T(...) custom-call(f32[32,8,128]{2,1,0:T(8,128)S(1)} %all_to_all.26.refs_0_, ...), custom_call_target="tpu_custom_call" | custom-call | tf_op jit(solution)/shard_map/pallas_call | solution.py:566
  43.2 10.0 %all_to_all.27.refs_0_ = f32[32,8,128]{2,1,0:T(8,128)S(1)} all-to-all(f32[32,8,128]{2,1,0:T(8,128)S(1)} %get-tuple-element.78), channel_id=1, replica_groups=mesh['gx'=4,'gy'=2,'gz'=4] {'gx','gy','gz'}, dimensions={0} | all-to-all | bytes 262144 | tf_op jit(solution)/shard_map/all_to_all | solution.py:576
  53.2 1.2 %shard_map.101 = (f32[8,1024]{1,0:T(8,128)S(1)}, f32[8,1024]{1,0:T(8,128)S(1)}, f32[8,1024]{1,0:T(8,128)S(1)}, f32[8,1024]{1,0:T(8,128)S(1)}, f32[8,1024]{1,0:T(...) custom-call(f32[32,8,128]{2,1,0:T(8,128)S(1)} %all_to_all.27.refs_0_, ...), custom_call_target="tpu_custom_call" | custom-call | tf_op jit(solution)/shard_map/pallas_call | solution.py:566
  54.4 8.9 %all_to_all.28.received = f32[32,1,128]{2,1,0:T(1,128)S(1)} all-to-all(f32[32,1,128]{2,1,0:T(1,128)S(1)} %get-tuple-element.87), channel_id=1, replica_groups=mesh['gx'=4,'gy'=2,'gz'=4] {'gx','gy','gz'}, dimensions={0} | all-to-all | bytes 32768 | tf_op jit(solution)/shard_map/all_to_all | solution.py:576
  63.3 0.8 %shard_map.102 = (f32[48,128]{1,0:T(8,128)}, f32[48,128]{1,0:T(8,128)}) custom-call(f32[32,1,128]{2,1,0:T(1,128)S(1)} %all_to_all.28.received, f32[8,1024]{1,0:T(8,128)S(1)} %get-tuple-element.88.r, f32[8,1024]{1,0:T(8,128)S(1)} %get-tuple-element.89.w, f32[8,1024]{1,0:T(8,128)S(1)} %get-tuple-element.90.p, f32[8,1024]{1,0:T(8,128)S(1)} %get-tuple-element.91.s, ...), custom_call_target="tpu_custom_call" | custom-call | tf_op jit(solution)/shard_map/pallas_call | solution.py:566
Async XLA Ops:
  2.4 15.9 %all-to-all-start = ((f32[32,5,2,128]{3,2,1,0:T(2,128)}), f32[32,5,2,128]{3,2,1,0:T(2,128)S(1)}, u32[]{:S(2)}, u32[]{:S(2)}) async-start(f32[32,5,2,128]{3,2,1,0:T(2,128)} %get-tuple-element.49), calls=%async_computation | async-start | bytes 327680 | tf_op jit(solution)/shard_map/all_to_all | solution.py:576
  18.2 1.4 %collective-permute-start = (f32[32,5,2,128]{3,2,1,0:T(2,128)S(1)}, f32[32,5,2,128]{3,2,1,0:T(2,128)S(1)}, u32[]{:S(2)}, u32[]{:S(2)}) collective-permute-start(f32[32,5,2,128]{3,2,1,0:T(2,128)S(1)} %all-to-all-done.received), channel_id=1, source_target_pairs={{0,1},{1,0},{2,3},{3,2},{4,5},{5,4},{6,7},{7,6},{8,9},{9,8},{10,11... | collective-permute-start | bytes 491528 | tf_op jit(solution)/shard_map/ppermute | solution.py:623
